TPU v7x, 512 devices: a whole 4x4x16 slice. The times are simulated.
512 devices in a mesh: fsdp: 16 (over x, y_lo, core), ctx: 32 (over y_hi, z).
Axes of the slice: x: 4, y: 4 (y_hi: 2, y_lo: 2; y = y_hi * 2 + y_lo), z: 16, core: 2. Of those that a mesh axis runs over, the one named last changes fastest.
Arguments:
- qkv: bfloat16 [4096, 3, 8192], P('ctx', None, 'fsdp'), may hold values from -6 to 6
- short_filter: float32 [3, 7, 8192], P(None, None, 'fsdp'), may hold values from -2 to 2
- long_filter: float32 [128, 8192], P('ctx', 'fsdp'), may hold values from -0.5 to 0.5
- proj: bfloat16 [8192, 4096], P('fsdp', 'ctx'), may hold values from -0.125 to 0.125
- out_grad: bfloat16 [4096, 4096], P('ctx', 'fsdp'), may hold values from -6 to 6
Outputs:
- layer_out: bfloat16 [4096, 4096], P('ctx', 'fsdp')
- grad_qkv: bfloat16 [4096, 3, 8192], P('ctx', None, 'fsdp')
- grad_short: float32 [3, 7, 8192], P(None, None, 'fsdp')
- grad_long: float32 [128, 8192], P('ctx', 'fsdp')
- grad_proj: float32 [8192, 4096], P('fsdp', 'ctx')
All inputs are finite; a program needn't handle non-finite values.
Results may differ from a plain program's by a relative error of at most 0.0049.
Values may be sent and summed in bfloat16 or wider, within the bound.
No kernel may reach another device: no remote copies, remote signals or barrier semaphores. Data moves between devices by JAX's collectives and lax.ppermute only.
A program may use at most 64 MiB of HBM per device.

v0:
```python
import jax
import jax.numpy as jnp
from jax import lax
from jax.sharding import PartitionSpec as P


def passed_along(value, axis, steps):
    count = lax.axis_size(axis)
    first, last = (max(0, -steps), min(count, count - steps))
    return lax.ppermute(value, axis, [(source, source + steps) for source in range(first, last)])


def depthwise(padded, kernel):
    result = lax.conv_general_dilated(
        padded[None],
        kernel[:, None, :],
        (1,),
        "VALID",
        dimension_numbers=("NWC", "WIO", "NWC"),
        feature_group_count=padded.shape[1],
        precision=lax.Precision.HIGHEST,
    )
    return result[0]


def local(qkv, short_filter, long_filter, proj, out_grad):
    rows_here = qkv.shape[0]
    channels = qkv.shape[2]
    reach_short = short_filter.shape[1]
    long_taps = lax.all_gather(long_filter, "ctx", axis=0, tiled=True)
    reach_long = long_taps.shape[0]
    inputs = qkv.reshape(rows_here, 3 * channels)
    input_rim = passed_along(inputs[rows_here - reach_short + 1 :], "ctx", 1)
    extended = jnp.concatenate([input_rim, inputs], axis=0).astype(jnp.float32)
    short_taps = jnp.transpose(short_filter, (1, 0, 2)).reshape(reach_short, 3 * channels)
    short_out = depthwise(extended, short_taps[::-1])
    query_side = short_out[:, :channels]
    key_side = short_out[:, channels : 2 * channels]
    value_side = short_out[:, 2 * channels :]
    product = key_side * value_side
    product_rim = passed_along(product[rows_here - reach_long + 1 :], "ctx", 1)
    product_ext = jnp.concatenate([product_rim, product], axis=0)
    long_mix = depthwise(product_ext, long_taps[::-1])
    gated_out = (query_side * long_mix).astype(jnp.bfloat16)
    everything = lax.all_gather(out_grad, "fsdp", axis=1, tiled=True)
    partial_value = jnp.dot(
        gated_out,
        lax.all_gather(proj, "ctx", axis=1, tiled=True),
        preferred_element_type=jnp.float32,
    )
    gated_grad = lax.dot_general(
        everything,
        lax.all_gather(proj, "ctx", axis=1, tiled=True),
        (((1,), (1,)), ((), ())),
        preferred_element_type=jnp.float32,
    )
    layer_out = lax.psum_scatter(partial_value, "fsdp", scatter_dimension=1, tiled=True).astype(
        jnp.bfloat16
    )
    columns_all = lax.all_to_all(everything, "ctx", split_axis=1, concat_axis=0, tiled=True)
    portion = jax.tree.map(lambda part: lax.all_gather(part, "ctx", axis=0, tiled=True), gated_out)
    grad_part = lax.slice_in_dim(columns_all, 0, portion.shape[0], axis=0)
    grad_proj = jnp.zeros((channels, columns_all.shape[1]), jnp.float32) + lax.dot_general(
        portion, grad_part, (((0,), (0,)), ((), ())), preferred_element_type=jnp.float32
    )
    query_grad = gated_grad * long_mix
    mixed_grad = gated_grad * query_side
    mixed_rim = passed_along(mixed_grad[: reach_long - 1], "ctx", -1)
    product_grad = depthwise(jnp.concatenate([mixed_grad, mixed_rim], axis=0), long_taps)
    long_part = depthwise(product_ext, mixed_grad)[::-1]
    short_grad = jnp.concatenate(
        [query_grad, product_grad * value_side, product_grad * key_side], axis=1
    )
    short_rim = passed_along(short_grad[: reach_short - 1], "ctx", -1)
    grad_inputs = depthwise(jnp.concatenate([short_grad, short_rim], axis=0), short_taps)
    grad_qkv = grad_inputs.reshape(rows_here, 3, channels).astype(jnp.bfloat16)
    short_part = jnp.transpose(
        depthwise(extended, short_grad)[::-1].reshape(reach_short, 3, channels), (1, 0, 2)
    )
    grad_long = lax.psum_scatter(long_part, "ctx", scatter_dimension=0, tiled=True)
    grad_short = lax.psum(short_part, "ctx")
    return (layer_out, grad_qkv, grad_short, grad_long, grad_proj)


def solution(mesh):
    in_specs = (
        P("ctx", None, "fsdp"),
        P(None, None, "fsdp"),
        P("ctx", "fsdp"),
        P("fsdp", "ctx"),
        P("ctx", "fsdp"),
    )
    out_specs = (
        P("ctx", "fsdp"),
        P("ctx", None, "fsdp"),
        P(None, None, "fsdp"),
        P("ctx", "fsdp"),
        P("fsdp", "ctx"),
    )
    return jax.shard_map(local, mesh=mesh, in_specs=in_specs, out_specs=out_specs, check_vma=False)
```

profile of v0, /device:TPU:6, one launch (start us, length us, event | category | flops | bytes accessed | tf_op | source)
XLA Modules:
  0.0 878.0 jit_solution(13519774245974245180)
XLA Ops:
  7.2 1.6 copy.59
  8.9 0.7 all-gather.5.cloned.1.call-update
  9.6 0.7 slice.24
  10.4 0.3 copy.53
  10.6 3.8 collective-permute-start
  14.5 1.2 copy.54
  15.7 0.3 rev.12
  16.1 6.7 collective-permute-done
  22.8 0.4 pad_maximum_fusion
  23.2 0.2 copy.55
  23.8 0.3 copy-done.3
  24.1 0.4 convolution_select_fusion
  24.6 0.5 copy.58
  25.3 29.1 %all-gather.7.cloned.1.call-done = bf16[128,4096]{0,1:T(8,128)(2,1)} async-done(((bf16[128,256]{0,1:T(8,128)(2,1)}), bf16[128,4096]{0,1:T(8,128)(2,1)}) %all-gather.7.cloned.1.call-update) | async-done | bytes 1048592 | tf_op jit(solution)/shard_map/all_gather | solution.py:45
  54.3 170.5 %all-gather.5.cloned.1.call-done = bf16[512,4096]{1,0:T(8,128)(2,1)} async-done(((bf16[512,128]{1,0:T(8,128)(2,1)}), bf16[512,4096]{1,0:T(8,128)(2,1)}) %all-gather.5.cloned.1.call-update) | async-done | bytes 4194320 | tf_op jit(solution)/shard_map/all_gather | solution.py:48
  224.8 4.0 slice_multiply_fusion.1
  228.8 1.3 collective-permute-start.2
  230.2 76.1 %all-gather = f32[32,4,512]{2,1,0:T(4,128)S(1)} all-gather(f32[1,4,512]{2,1,0:T(4,128)S(1)} %bitcast.70), channel_id=1, replica_groups=mesh['fsdp'=16,'ctx'=32] {'ctx'}, dimensions={0}, use_global_device_ids=true | all-gather | bytes 270336 | tf_op jit(solution)/shard_map/all_gather | solution.py:30
  306.2 0.3 broadcast_in_dim.34
  306.6 2.8 fusion.17
  309.6 2.0 collective-permute-start.1
  312.0 2.7 collective-permute-done.1
  314.8 1.0 pad_maximum_fusion.2
  315.7 0.4 broadcast_in_dim.31
  316.1 3.8 fusion.31
  319.9 2.8 fusion.21
  322.8 1.3 rev.15
  324.3 4.3 fusion.32
  328.7 0.5 all-gather.9.cloned.1.call-update
  329.2 21.7 %all-to-all-start = ((bf16[128,32,128]{0,2,1:T(8,128)(2,1)}), bf16[128,32,128]{0,2,1:T(8,128)(2,1)S(1)}, u32[]{:S(2)}, u32[]{:S(2)}) async-start(bf16[128,32,128]{0,2,1:T(8,128)(2,1)} %bitcast.16), calls=%async_computation.1 | async-start | bytes 2097152 | tf_op jit(solution)/shard_map/all_to_all | solution.py:60
  350.9 1.3 dynamic-slice
  352.8 32.0 %all-to-all-done = bf16[128,32,128]{0,2,1:T(8,128)(2,1)S(1)} async-done(((bf16[128,32,128]{0,2,1:T(8,128)(2,1)}), bf16[128,32,128]{0,2,1:T(8,128)(2,1)S(1)}, u32[]{:S(2)}, u32[]{:S(2)}) %all-to-all-start) | async-done | bytes 1048608 | tf_op jit(solution)/shard_map/all_to_all | solution.py:60
  384.8 0.7 copy.69
  385.7 1.3 collective-permute-start.3
  387.0 1.7 fusion.6
  388.8 0.3 rev.14
  389.1 146.4 %psum.7 = f32[3,7,512]{2,0,1:T(4,128)S(1)} all-reduce(f32[3,7,512]{2,0,1:T(4,128)S(1)} %bitcast.66), channel_id=1, replica_groups=mesh['fsdp'=16,'ctx'=32] {'ctx'}, use_global_device_ids=true, to_apply=%region_1.0 | all-reduce | flops 10752 | bytes 86016 | tf_op jit(solution)/shard_map/psum | solution.py:81
  535.5 0.6 copy.71
  536.3 1.0 reshape.36
  537.4 0.4 fusion
  538.2 0.2 copy.65
  538.4 0.9 copy.70
  539.3 95.3 %all-reduce.3.cloned.1.call-done = f32[128,512]{1,0:T(8,128)} async-done(((f32[128,512]{1,0:T(8,128)}), f32[128,512]{1,0:T(8,128)}) %all-reduce.3.cloned.1.call-update) | async-done | bytes 262160
  634.6 1.3 constant_dynamic-slice_fusion
  636.0 58.8 %reduce-scatter.2.cloned.1.call-done = f32[128,256]{1,0:T(8,128)} async-done(((f32[128,4096]{1,0:T(8,128)}), f32[128,256]{1,0:T(8,128)}) %reduce-scatter.2.cloned.1.call-update) | async-done | bytes 131088 | tf_op jit(solution)/shard_map/reduce_scatter | solution.py:57
  694.8 1.5 convert_element_type.14
  696.3 170.9 %all-gather.9.cloned.1.call-done = bf16[4096,512]{1,0:T(8,128)(2,1)} async-done(((bf16[128,512]{1,0:T(8,128)(2,1)}), bf16[4096,512]{1,0:T(8,128)(2,1)}) %all-gather.9.cloned.1.call-update) | async-done | bytes 4194320 | tf_op jit(solution)/shard_map/all_gather | solution.py:61
  867.3 4.2 fusion.33
  (43 shorter events, 2.3 us)
Async XLA Ops:
  7.2 8.5 copy-start.1
  7.2 47.2 %all-gather.7.cloned.1.call-start = ((), (), s32[]{:S(2)}) async-start(), calls=%async_computation.4 | async-start | bytes 1114112 | tf_op jit(solution)/shard_map/all_gather | solution.py:45
  8.8 216.0 %all-gather.5.cloned.1.call-start = ((), (), s32[]{:S(2)}) async-start(), calls=%async_computation.2 | async-start | bytes 4325376 | tf_op jit(solution)/shard_map/all_gather | solution.py:48
  9.6 625.1 %all-reduce.3.cloned.1.call-start = ((), (), s32[]{:S(2)}) async-start(), calls=%async_computation.6 | async-start | bytes 524288
  10.6 12.2 %collective-permute-start = (bf16[6,1536]{0,1:T(8,128)(2,1)S(1)}, bf16[6,1536]{0,1:T(8,128)(2,1)S(1)}, u32[]{:S(2)}, u32[]{:S(2)}) collective-permute-start(bf16[6,1536]{0,1:T(8,128)(2,1)S(1)} %bitcast.65), channel_id=1, source_target_pairs={{0,1},{1,2},{2,3},{3,4},{4,5},{5,6},{6,7},{7,8},{8,9},{9,10},{10,1... | collective-permute-start | bytes 55304 | tf_op jit(solution)/shard_map/ppermute | solution.py:10
  23.4 0.7 copy-start.3
  25.3 204.9 %copy-start.2 = (f32[4,512]{1,0:T(4,128)S(1)}, f32[4,512]{1,0:T(4,128)}, u32[]{:S(2)}) copy-start(f32[4,512]{1,0:T(4,128)} %param.7) | copy-start | bytes 24580
  228.8 77.7 %collective-permute-start.2 = (f32[127,512]{1,0:T(8,128)S(1)}, f32[127,512]{1,0:T(8,128)S(1)}, u32[]{:S(2)}, u32[]{:S(2)}) collective-permute-start(f32[127,512]{1,0:T(8,128)S(1)} %bitcast.62), channel_id=1, source_target_pairs={{1,0},{2,1},{3,2},{4,3},{5,4},{6,5},{7,6},{8,7},{9,8},{10,9},{11,1... | collective-permute-start | bytes 780296 | tf_op jit(solution)/shard_map/ppermute | solution.py:10
  309.6 5.2 collective-permute-start.1
  324.2 370.6 %reduce-scatter.2.cloned.1.call-start = ((), (), s32[]{:S(2)}) async-start(), calls=%async_computation.3 | async-start | bytes 2228224 | tf_op jit(solution)/shard_map/reduce_scatter | solution.py:57
  324.3 4.3 copy-start
  328.6 538.6 %all-gather.9.cloned.1.call-start = ((), (), s32[]{:S(2)}) async-start(), calls=%async_computation.5 | async-start | bytes 4325376 | tf_op jit(solution)/shard_map/all_gather | solution.py:61
  329.2 55.6 %all-to-all-start = ((bf16[128,32,128]{0,2,1:T(8,128)(2,1)}), bf16[128,32,128]{0,2,1:T(8,128)(2,1)S(1)}, u32[]{:S(2)}, u32[]{:S(2)}) async-start(bf16[128,32,128]{0,2,1:T(8,128)(2,1)} %bitcast.16), calls=%async_computation.1 | async-start | bytes 2097152 | tf_op jit(solution)/shard_map/all_to_all | solution.py:60
  385.7 150.4 %collective-permute-start.3 = (f32[6,1536]{1,0:T(8,128)S(1)}, f32[6,1536]{1,0:T(8,128)S(1)}, u32[]{:S(2)}, u32[]{:S(2)}) collective-permute-start(f32[6,1536]{1,0:T(8,128)S(1)} %slice.43), channel_id=1, source_target_pairs={{1,0},{2,1},{3,2},{4,3},{5,4},{6,5},{7,6},{8,7},{9,8},{10,9},{11,1... | collective-permute-start | bytes 110600 | tf_op jit(solution)/shard_map/ppermute | solution.py:10
Sparse Core Ops, SparseCore 0:
  10.7 43.5 all-gather.6
  57.3 167.5 all-gather.4
  324.3 310.3 all-reduce.2
  637.6 57.1 reduce-scatter.1
  698.2 169.0 all-gather.8
where the time goes:
time: 879 us; the launch traced here: 878 us
  waiting for transfers between devices  567 us (65%)
  blocking collectives  222 us (25%)
  starting transfers between devices  30.3 us (3%)
  matrix products  24.6 us (3%)
  local copies, waits for them, and re-layouts  15.1 us (2%)
  between operations  14.8 us (2%)
    all_gather x1, waiting for transfers between devices, local(): lax.all_gather(part, 'ctx', axis=0, tiled=True)  171 us
    all_gather x1, waiting for transfers between devices, local(): lax.all_gather(proj, 'ctx', axis=1, tiled=True)  170 us
    psum x1, blocking collectives, local(): grad_short = lax.psum(short_part, 'ctx')  146 us
    unnamed x6, waiting for transfers between devices  96.6 us
    all_gather x1, blocking collectives, local(): long_taps = lax.all_gather(long_filter, 'ctx', axis=0, tiled=True)  76.1 us
    reduce_scatter x1, waiting for transfers between devices, local(): lax.psum_scatter(partial_value, 'fsdp', scatter_dimension=1, tiled=True)  58.8 us
    all_to_all x1, waiting for transfers between devices, local(): lax.all_to_all(everything, 'ctx', split_axis=1, concat_axis=0, tiled=True)  32 us
    all_gather x1, waiting for transfers between devices, local(): everything = lax.all_gather(out_grad, 'fsdp', axis=1, tiled=True)  29.1 us
  transfers between devices with their start and end apart: 10, of which 8 were waited for; matrix products, arithmetic and copies ran while one was open for 2% of the time, Pallas kernels for 0%

commit v1 on v0

v1 whole, which is shorter than its diff:
```python
import jax
import jax.numpy as jnp
from jax import lax
from jax.sharding import Mesh, PartitionSpec as P

F32 = jnp.float32
BF16 = jnp.bfloat16
AXES = ("x", "yl", "co", "yh", "z")
SIZES = (4, 2, 2, 2, 16)
CTX = ("yh", "z")
FSDP = ("x", "yl", "co")


def passed_along(value, steps):
    count = 32
    first, last = (max(0, -steps), min(count, count - steps))
    return lax.ppermute(value, CTX, [(source, source + steps) for source in range(first, last)])


def swapped(value, axis):
    return lax.ppermute(value, axis, [(0, 1), (1, 0)])


def ordered(index, own, other):
    first = jnp.where(index == 0, own, other)
    second = jnp.where(index == 0, other, own)
    return jnp.stack([first, second])


def depthwise(padded, kernel):
    result = lax.conv_general_dilated(
        padded[None],
        kernel[:, None, :],
        (1,),
        "VALID",
        dimension_numbers=("NWC", "WIO", "NWC"),
        feature_group_count=padded.shape[1],
        precision=lax.Precision.HIGHEST,
    )
    return result[0]


def owner_pairs():
    pairs = []
    for x in range(4):
        for rest in range(4):
            for yh in range(2):
                for z in range(16):
                    source = ((x * 4 + rest) * 2 + yh) * 16 + z
                    target = (((2 * yh + x % 2) * 4 + rest) * 2 + x // 2) * 16 + z
                    pairs.append((source, target))
    return pairs


def local(qkv, short_filter, long_filter, proj, out_grad):
    rows = qkv.shape[0]
    channels = qkv.shape[2]
    reach_short = short_filter.shape[1]
    taps_here = long_filter.shape[0]
    yh = lax.axis_index("yh")
    co = lax.axis_index("co")

    taps_high = lax.reduce_precision(long_filter, exponent_bits=8, mantissa_bits=7)
    taps_low = (long_filter - taps_high).astype(BF16)
    taps_high = taps_high.astype(BF16)
    pack_rows = 2 * taps_here * channels // 128
    pack = jnp.concatenate([taps_high, taps_low], axis=0).reshape(pack_rows, 128)
    gathered = lax.all_gather(jnp.concatenate([proj, pack], axis=0), "z", axis=1, tiled=True)
    proj_half = gathered[:channels]
    taps_pack = gathered[channels:].reshape(2, taps_here, channels // 128, 16, 128)
    taps_pack = jnp.transpose(taps_pack, (0, 3, 1, 2, 4)).reshape(2, 16 * taps_here, channels)
    taps_own = taps_pack[0].astype(F32) + taps_pack[1].astype(F32)
    taps_other = swapped(taps_own, "yh")
    long_taps = ordered(yh, taps_own, taps_other).reshape(32 * taps_here, channels)
    reach_long = long_taps.shape[0]

    along_x = lax.all_gather(out_grad, "x", axis=0, tiled=False).reshape(2, 2, rows, out_grad.shape[1])
    kept = lax.dynamic_index_in_dim(along_x, yh, 0, keepdims=False)
    given = lax.dynamic_index_in_dim(along_x, 1 - yh, 0, keepdims=False)
    both = ordered(yh, kept, swapped(given, "yh"))
    along_y = lax.all_gather(both, "yl", axis=0, tiled=False)
    along_c = ordered(co, along_y, swapped(along_y, "co"))
    grads = jnp.transpose(along_c, (2, 4, 3, 1, 0, 5)).reshape(2 * rows, 8 * out_grad.shape[1])

    inputs = qkv.reshape(rows, 3 * channels)
    input_rim = passed_along(inputs[rows - reach_short + 1 :], 1)
    extended = jnp.concatenate([input_rim, inputs], axis=0).astype(F32)
    short_taps = jnp.transpose(short_filter, (1, 0, 2)).reshape(reach_short, 3 * channels)
    short_out = depthwise(extended, short_taps[::-1])
    query_side = short_out[:, :channels]
    key_side = short_out[:, channels : 2 * channels]
    value_side = short_out[:, 2 * channels :]
    product = key_side * value_side
    product_rim = passed_along(product[rows - reach_long + 1 :], 1)
    product_ext = jnp.concatenate([product_rim, product], axis=0)

    grad_part = lax.dot_general(grads, proj_half, (((1,), (1,)), ((), ())), preferred_element_type=F32)
    grad_part = grad_part.reshape(2, rows, channels)
    part_kept = lax.dynamic_index_in_dim(grad_part, yh, 0, keepdims=False)
    part_given = lax.dynamic_index_in_dim(grad_part, 1 - yh, 0, keepdims=False)
    gated_grad = part_kept + swapped(part_given, "yh")

    long_mix = depthwise(product_ext, long_taps[::-1])
    gated_out = (query_side * long_mix).astype(BF16)
    gated_both = ordered(yh, gated_out, swapped(gated_out, "yh")).reshape(2 * rows, channels)

    out_part = jnp.dot(gated_both, proj_half, preferred_element_type=F32)
    out_part = out_part.reshape(2, rows, 2, 2, 2, out_grad.shape[1])
    out_part = jnp.transpose(out_part, (4, 0, 2, 3, 1, 5))
    out_kept = lax.dynamic_index_in_dim(out_part, co, 0, keepdims=False)
    out_given = lax.dynamic_index_in_dim(out_part, 1 - co, 0, keepdims=False)
    out_chip = (out_kept + swapped(out_given, "co")).astype(BF16).reshape(8, rows, out_grad.shape[1])
    out_terms = lax.all_to_all(out_chip, ("x", "yl"), 0, 0, tiled=True)
    out_sum = jnp.sum(out_terms.astype(F32), axis=0).astype(BF16)
    layer_out = lax.ppermute(out_sum, AXES, owner_pairs())

    proj_part = lax.dot_general(gated_both, grads, (((0,), (0,)), ((), ())), preferred_element_type=F32)
    grad_proj = lax.psum_scatter(proj_part, "z", scatter_dimension=1, tiled=True)

    query_grad = gated_grad * long_mix
    mixed_grad = gated_grad * query_side
    mixed_rim = passed_along(mixed_grad[: reach_long - 1], -1)
    product_grad = depthwise(jnp.concatenate([mixed_grad, mixed_rim], axis=0), long_taps)
    long_part = depthwise(product_ext, mixed_grad)[::-1].reshape(2, 16, taps_here, channels)
    short_grad = jnp.concatenate([query_grad, product_grad * value_side, product_grad * key_side], axis=1)
    short_rim = passed_along(short_grad[: reach_short - 1], -1)
    grad_inputs = depthwise(jnp.concatenate([short_grad, short_rim], axis=0), short_taps)
    grad_qkv = grad_inputs.reshape(rows, 3, channels).astype(BF16)
    short_part = depthwise(extended, short_grad)[::-1]

    short_rows = short_part.reshape(reach_short * 3, channels)
    short_rows = jnp.pad(short_rows, ((0, 32 - reach_short * 3), (0, 0))).reshape(16, 2, channels)
    long_kept = lax.dynamic_index_in_dim(long_part, yh, 0, keepdims=False)
    long_given = lax.dynamic_index_in_dim(long_part, 1 - yh, 0, keepdims=False)
    terms_given = jnp.concatenate([long_given, short_rows], axis=1)
    terms_kept = jnp.concatenate([long_kept, short_rows], axis=1)
    terms = terms_kept + swapped(terms_given, "yh")
    sums = jnp.sum(lax.all_to_all(terms, "z", 0, 0, tiled=True), axis=0)
    grad_long = sums[:taps_here]
    short_copies = jnp.broadcast_to(sums[None, taps_here:], (16, 2, channels))
    short_sum = lax.all_to_all(short_copies, "z", 0, 0, tiled=True).reshape(32, channels)[: 3 * reach_short]
    grad_short = jnp.transpose(short_sum.reshape(reach_short, 3, channels), (1, 0, 2))
    return (layer_out, grad_qkv, grad_short, grad_long, grad_proj)


def solution(mesh):
    fine = Mesh(mesh.devices.reshape(SIZES), AXES)
    in_specs = (
        P(CTX, None, FSDP),
        P(None, None, FSDP),
        P(CTX, FSDP),
        P(FSDP, CTX),
        P(CTX, FSDP),
    )
    out_specs = (
        P(CTX, FSDP),
        P(CTX, None, FSDP),
        P(None, None, FSDP),
        P(CTX, FSDP),
        P(FSDP, CTX),
    )
    return jax.shard_map(local, mesh=fine, in_specs=in_specs, out_specs=out_specs, check_vma=False)
```

time: 879 us -> 239 us (0.27)
  waiting for transfers between devices: 567 us -> 85.3 us
  blocking collectives: 222 us -> 20 us
  starting transfers between devices: 30.3 us -> 61.7 us
  local copies, waits for them, and re-layouts: 15.1 us -> 24.1 us
    all_gather x3 -> x1, waiting for transfers between devices: 370 us -> 36.8 us  [local(): lax.all_gather(jnp.concatenate([proj, pack], axis=0), 'z', axis=1, tiled=...]
    psum x1 -> x0, blocking collectives: 146 us -> none  [local(): grad_short = lax.psum(short_part, 'ctx')]
    unnamed x6 -> x2, waiting for transfers between devices: 96.6 us -> 0.03 us
    reduce_scatter x1, waiting for transfers between devices: 58.8 us -> 0.01 us  [local(): lax.psum_scatter(proj_part, 'z', scatter_dimension=1, tiled=True)]
    all_gather x1 -> x2, blocking collectives: 76.1 us -> 20 us  [the longest x1 13 us: local(): lax.all_gather(out_grad, 'x', axis=0, tiled=False)]
    ppermute x4 -> x12, starting transfers between devices: 8.46 us -> 41.4 us  [the longest x7 25.2 us: swapped(): return lax.ppermute(value, axis, [(0, 1), (1, 0)])]
    ppermute x4 -> x12, waiting for transfers between devices: 9.47 us -> 23.9 us  [the longest x4 13.9 us: passed_along(): lax.ppermute(value, CTX, [(source, source + steps) for source in range(fi...]
    all_to_all x1 -> x3, waiting for transfers between devices: 32 us -> 24.6 us  [the longest x1 17.8 us: local(): sums = jnp.sum(lax.all_to_all(terms, 'z', 0, 0, tiled=True), axis=0)]
  transfers between devices with their start and end apart: 10 -> 17, of which waited for: 8 -> 9; matrix products, arithmetic and copies ran while one was open for 2% -> 19% of each run, Pallas kernels for 0% -> 0%
where the time goes in v1:
time: 239 us; the launch traced here: 236 us
  waiting for transfers between devices  85.3 us (36%)
  starting transfers between devices  61.7 us (26%)
  local copies, waits for them, and re-layouts  24.1 us (10%)
  matrix products  20.1 us (8%)
  blocking collectives  20 us (8%)
  between operations  14.9 us (6%)
  other arithmetic  10 us (4%)
    all_gather x1, waiting for transfers between devices, local(): lax.all_gather(jnp.concatenate([proj, pack], axis=0), 'z', axis=1, tiled=...  36.8 us
    ppermute x7, starting transfers between devices, swapped(): return lax.ppermute(value, axis, [(0, 1), (1, 0)])  25.2 us
    all_to_all x1, waiting for transfers between devices, local(): sums = jnp.sum(lax.all_to_all(terms, 'z', 0, 0, tiled=True), axis=0)  17.8 us
    ppermute x4, waiting for transfers between devices, passed_along(): lax.ppermute(value, CTX, [(source, source + steps) for source in range(fi...  13.9 us
    all_gather x1, blocking collectives, local(): lax.all_gather(out_grad, 'x', axis=0, tiled=False)  13 us
    conv_general_dilated x6, matrix products, depthwise(): lax.conv_general_dilated(padded[None], kernel[:, None, :], (1,), 'VALID',...  12.7 us
    ppermute x4, starting transfers between devices, passed_along(): lax.ppermute(value, CTX, [(source, source + steps) for source in range(fi...  10.3 us
    ppermute x7, waiting for transfers between devices, swapped(): return lax.ppermute(value, axis, [(0, 1), (1, 0)])  9.92 us
  transfers between devices with their start and end apart: 17, of which 9 were waited for; matrix products, arithmetic and copies ran while one was open for 19% of the time, Pallas kernels for 0%

profile of v1, /device:TPU:6, one launch (start us, length us, event | category | flops | bytes accessed | tf_op | source)
XLA Modules:
  0.0 236.1 jit_solution(7519381920856031967)
XLA Ops:
  8.0 1.6 pad_maximum_fusion.8
  10.6 3.8 %collective-permute-start = (bf16[6,1536]{0,1:T(8,128)(2,1)S(1)}, bf16[6,1536]{0,1:T(8,128)(2,1)S(1)}, u32[]{:S(2)}, u32[]{:S(2)}) collective-permute-start(bf16[6,1536]{0,1:T(8,128)(2,1)S(1)} %bitcast.150), channel_id=1, source_target_pairs={{0,1},{1,2},{2,3},{3,4},{4,5},{5,6},{6,7},{7,8},{8,9},{9,10},{10,1... | collective-permute-start | bytes 55304 | tf_op jit(solution)/shard_map/ppermute | solution.py:17
  14.5 13.0 %all-gather = bf16[512,256]{1,0:T(8,128)(2,1)S(1)} all-gather(bf16[128,256]{1,0:T(8,128)(2,1)} %param.9), channel_id=2, replica_groups=mesh['x'=4,'yl'=2,'co'=2,'yh'=2,'z'=16] {'x'}, dimensions={0}, use_global_device_ids=true | all-gather | bytes 327680 | tf_op jit(solution)/shard_map/all_gather | solution.py:77
  27.5 4.8 %collective-permute-start.6 = (bf16[2,128,256]{2,1,0:T(8,128)(2,1)S(1)}, bf16[2,128,256]{2,1,0:T(8,128)(2,1)S(1)}, u32[]{:S(2)}, u32[]{:S(2)}) collective-permute-start(bf16[2,128,256]{2,1,0:T(8,128)(2,1)S(1)} %dynamic-slice_bitcast_fusion.4), channel_id=1, source_target_pairs={{0,16},{16,0},{1,17},{17,1},{2,18},{18,2},{3,19},{19,3},{4,20},{20... | collective-permute-start | bytes 393224 | tf_op jit(solution)/shard_map/ppermute | solution.py:21
  32.2 1.2 copy.63
  36.5 7.0 %all-gather.1 = bf16[4,2,128,256]{3,2,1,0:T(8,128)(2,1)S(1)} all-gather(bf16[2,2,128,256]{3,2,1,0:T(8,128)(2,1)S(1)} %pad_maximum_fusion.7), channel_id=3, replica_groups=mesh['x'=4,'yl'=2,'co'=2,'yh'=2,'z'=16] {'yl'}, dimensions={0}, use_global_device_ids=true | all-gather | bytes 786432 | tf_op jit(solution)/shard_map/all_gather | solution.py:81
  43.5 1.9 collective-permute-start.7
  45.5 3.8 %collective-permute-start.1 = (f32[127,512]{1,0:T(8,128)S(1)}, f32[127,512]{1,0:T(8,128)S(1)}, u32[]{:S(2)}, u32[]{:S(2)}) collective-permute-start(f32[127,512]{1,0:T(8,128)S(1)} %slice.71), channel_id=1, source_target_pairs={{0,1},{1,2},{2,3},{3,4},{4,5},{5,6},{6,7},{7,8},{8,9},{9,10},{10,1... | collective-permute-start | bytes 780296 | tf_op jit(solution)/shard_map/ppermute | solution.py:17
  49.4 9.1 %collective-permute-done.1 = f32[127,512]{1,0:T(8,128)S(1)} collective-permute-done((f32[127,512]{1,0:T(8,128)S(1)}, f32[127,512]{1,0:T(8,128)S(1)}, u32[]{:S(2)}, u32[]{:S(2)}) %collective-permute-start.1) | collective-permute-done | bytes 260128 | tf_op jit(solution)/shard_map/ppermute | solution.py:17
  58.6 1.1 broadcast_in_dim.34
  59.9 1.1 copy.71
  61.8 36.8 %all-gather.4.cloned.1.call-done = bf16[544,2048]{1,0:T(8,128)(2,1)} async-done(((bf16[544,128]{1,0:T(8,128)(2,1)}), bf16[544,2048]{1,0:T(8,128)(2,1)}) %all-gather.4.cloned.1.call-update) | async-done | bytes 2228240 | tf_op jit(solution)/shard_map/all_gather | solution.py:68
  98.6 0.9 slice_bitcast_fusion.2
  99.6 3.1 %collective-permute-start.2 = (f32[64,512]{1,0:T(8,128)S(1)}, f32[64,512]{1,0:T(8,128)S(1)}, u32[]{:S(2)}, u32[]{:S(2)}) collective-permute-start(f32[64,512]{1,0:T(8,128)S(1)} %bitcast.153), channel_id=1, source_target_pairs={{0,16},{16,0},{1,17},{17,1},{2,18},{18,2},{3,19},{19,3},{4,20},{20... | collective-permute-start | bytes 393224 | tf_op jit(solution)/shard_map/ppermute | solution.py:21
  102.8 2.3 fusion.1
  105.9 4.2 %collective-permute-start.8 = (f32[128,512]{1,0:T(8,128)}, f32[128,512]{1,0:T(8,128)S(1)}, u32[]{:S(2)}, u32[]{:S(2)}) collective-permute-start(f32[128,512]{1,0:T(8,128)} %dynamic-slice_bitcast_fusion.1), channel_id=1, source_target_pairs={{0,16},{16,0},{1,17},{17,1},{2,18},{18,2},{3,19},{19,3},{4,20},{20... | collective-permute-start | bytes 786440 | tf_op jit(solution)/shard_map/ppermute | solution.py:21
  110.5 3.7 %fusion.41 = f32[1,128,512]{2,0,1:T(1,128)S(1)} fusion(f32[1,255,512]{2,0,1:T(1,128)S(1)} %copy-done.11, f32[128,1,512]{2,1,0:T(1,128)S(1)} %broadcast_in_dim.35), kind=kOutput, calls=%fused_computation.87 | convolution fusion | flops 100663296 | bytes 1046528 | tf_op jit(solution)/shard_map/conv_general_dilated | solution.py:31
  114.2 1.6 collective-permute-done.8
  116.7 4.2 %collective-permute-start.3 = (bf16[128,512]{1,0:T(8,128)(2,1)S(1)}, bf16[128,512]{1,0:T(8,128)(2,1)}, u32[]{:S(2)}, u32[]{:S(2)}) collective-permute-start(bf16[128,512]{1,0:T(8,128)(2,1)S(1)} %get-tuple-element.28), channel_id=1, source_target_pairs={{0,16},{16,0},{1,17},{17,1},{2,18},{18,2},{3,19},{19,3},{4,20},{20... | collective-permute-start | bytes 393224 | tf_op jit(solution)/shard_map/ppermute | solution.py:21
  121.7 3.4 %collective-permute-done.3 = bf16[128,512]{1,0:T(8,128)(2,1)} collective-permute-done((bf16[128,512]{1,0:T(8,128)(2,1)S(1)}, bf16[128,512]{1,0:T(8,128)(2,1)}, u32[]{:S(2)}, u32[]{:S(2)}) %collective-permute-start.3) | collective-permute-done | bytes 131104 | tf_op jit(solution)/shard_map/ppermute | solution.py:21
  125.1 1.0 select_bitcast_fusion.3
  126.1 2.7 %fusion.42 = f32[512,2048]{1,0:T(8,128)} fusion(bf16[256,512]{1,0:T(8,128)(2,1)S(1)} %bitcast.140, bf16[256,2048]{1,0:T(8,128)(2,1)S(1)} %reshape.83), kind=kOutput, calls=%fused_computation.88 | convolution fusion | flops 536870912 | bytes 5505024 | tf_op jit(solution)/shard_map/dot_general | solution.py:117
  128.9 1.7 slice_bitcast_fusion
  130.6 2.6 %copy.69 = bf16[2048,512]{1,0:T(8,128)(2,1)} copy(bf16[2048,512]{0,1:T(8,128)(2,1)S(1)} %slice_bitcast_fusion) | data formatting | bytes 4194304 | tf_op jit(solution)/shard_map/dot_general | solution.py:107
  133.2 1.0 broadcast_in_dim_reshape.6
  134.2 3.6 %fusion.28 = f32[1,128,512]{2,0,1:T(1,128)S(1)} fusion(f32[1,255,512]{2,0,1:T(1,128)} %broadcast_in_dim.34, f32[128,1,512]{2,0,1:T(8,128)} %bitcast.40), kind=kOutput, calls=%fused_computation.53 | convolution fusion | flops 100663296 | bytes 1046528 | tf_op jit(solution)/shard_map/conv_general_dilated | solution.py:31
  138.1 1.3 collective-permute-start.9
  140.2 2.3 fusion.26
  142.5 1.1 dynamic-slice_bitcast_fusion
  143.7 2.1 collective-permute-start.4
  145.8 4.8 %collective-permute-done.9 = f32[127,512]{1,0:T(8,128)S(1)} collective-permute-done((f32[127,512]{1,0:T(8,128)}, f32[127,512]{1,0:T(8,128)S(1)}, u32[]{:S(2)}, u32[]{:S(2)}) %collective-permute-start.9) | collective-permute-done | bytes 260128 | tf_op jit(solution)/shard_map/ppermute | solution.py:17
  150.6 1.0 maximum_bitcast_fusion.2
  151.6 2.8 %fusion.21 = f32[1,128,512]{2,0,1:T(1,128)S(1)} fusion(f32[128,1,512]{2,1,0:T(1,128)S(1)} %copy-done.12, f32[1,255,512]{2,1,0:T(8,128)S(1)} %maximum_bitcast_fusion.2), kind=kOutput, calls=%fused_computation.35 | convolution fusion | flops 100663296 | bytes 1046528 | tf_op jit(solution)/shard_map/conv_general_dilated | solution.py:31
  154.5 1.0 fusion.40
  155.5 1.7 fusion.10
  157.7 4.9 %collective-permute-start.11 = (f32[16,6,512]{2,1,0:T(8,128)S(1)}, f32[16,6,512]{2,1,0:T(8,128)S(1)}, u32[]{:S(2)}, u32[]{:S(2)}) collective-permute-start(f32[16,6,512]{2,1,0:T(8,128)S(1)} %pad_maximum_fusion.3), channel_id=1, source_target_pairs={{0,16},{16,0},{1,17},{17,1},{2,18},{18,2},{3,19},{19,3},{4,20},{20... | collective-permute-start | bytes 589832 | tf_op jit(solution)/shard_map/ppermute | solution.py:21
  162.6 4.8 %collective-permute-done.11 = f32[16,6,512]{2,1,0:T(8,128)S(1)} collective-permute-done((f32[16,6,512]{2,1,0:T(8,128)S(1)}, f32[16,6,512]{2,1,0:T(8,128)S(1)}, u32[]{:S(2)}, u32[]{:S(2)}) %collective-permute-start.11) | collective-permute-done | bytes 196640 | tf_op jit(solution)/shard_map/ppermute | solution.py:21
  168.2 8.9 %all-to-all-start.1 = ((f32[16,6,512]{2,1,0:T(8,128)}), f32[16,6,512]{2,1,0:T(8,128)S(1)}, u32[]{:S(2)}, u32[]{:S(2)}) async-start(f32[16,6,512]{2,1,0:T(8,128)} %fusion.24), calls=%async_computation.1 | async-start | bytes 524288 | tf_op jit(solution)/shard_map/all_to_all | solution.py:138
  177.2 2.2 fusion.9
  179.4 17.8 %all-to-all-done.1 = f32[16,6,512]{2,1,0:T(8,128)S(1)} async-done(((f32[16,6,512]{2,1,0:T(8,128)}), f32[16,6,512]{2,1,0:T(8,128)S(1)}, u32[]{:S(2)}, u32[]{:S(2)}) %all-to-all-start.1) | async-done | bytes 196640 | tf_op jit(solution)/shard_map/all_to_all | solution.py:138
  197.1 6.2 %all-to-all-start = ((bf16[8,128,256]{2,1,0:T(8,128)(2,1)}), bf16[8,128,256]{2,1,0:T(8,128)(2,1)S(1)}, u32[]{:S(2)}, u32[]{:S(2)}) async-start(bf16[8,128,256]{2,1,0:T(8,128)(2,1)} %bitcast.22), calls=%async_computation | async-start | bytes 1048576 | tf_op jit(solution)/shard_map/all_to_all | solution.py:113
  204.1 1.3 collective-permute-start.10
  205.5 3.9 %all-to-all-done = bf16[8,128,256]{2,1,0:T(8,128)(2,1)S(1)} async-done(((bf16[8,128,256]{2,1,0:T(8,128)(2,1)}), bf16[8,128,256]{2,1,0:T(8,128)(2,1)S(1)}, u32[]{:S(2)}, u32[]{:S(2)}) %all-to-all-start) | async-done | bytes 524320 | tf_op jit(solution)/shard_map/all_to_all | solution.py:113
  210.0 5.0 %all-to-all-start.2 = ((f32[16,2,512]{2,1,0:T(2,128)}), f32[16,2,512]{2,1,0:T(2,128)S(1)}, u32[]{:S(2)}, u32[]{:S(2)}) async-start(f32[16,2,512]{2,1,0:T(2,128)} %broadcast_in_dim.40), calls=%async_computation.2 | async-start | bytes 131072 | tf_op jit(solution)/shard_map/all_to_all | solution.py:141
  215.2 1.0 reshape.93
  216.4 5.9 %collective-permute-start.5 = (bf16[128,256]{1,0:T(8,128)(2,1)S(1)}, bf16[128,256]{1,0:T(8,128)(2,1)S(1)}, u32[]{:S(2)}, u32[]{:S(2)}) collective-permute-start(bf16[128,256]{1,0:T(8,128)(2,1)S(1)} %reduce_sum.21), channel_id=1, source_target_pairs={{0,0},{1,1},{2,2},{3,3},{4,4},{5,5},{6,6},{7,7},{8,8},{9,9},{10,10... | collective-permute-start | bytes 196616 | tf_op jit(solution)/shard_map/ppermute | solution.py:115
  223.4 0.9 copy.82
  224.9 3.0 %all-to-all-done.2 = f32[16,2,512]{2,1,0:T(2,128)S(1)} async-done(((f32[16,2,512]{2,1,0:T(2,128)}), f32[16,2,512]{2,1,0:T(2,128)S(1)}, u32[]{:S(2)}, u32[]{:S(2)}) %all-to-all-start.2) | async-done | bytes 65568 | tf_op jit(solution)/shard_map/all_to_all | solution.py:141
  (114 shorter events, 15.7 us)
Async XLA Ops:
  7.2 26.3 %copy-start.13 = (f32[3,7,512]{2,1,0:T(8,128)S(1)}, f32[3,7,512]{2,1,0:T(8,128)}, u32[]{:S(2)}) copy-start(f32[3,7,512]{2,1,0:T(8,128)} %param.6) | copy-start | bytes 129028
  7.2 91.4 %all-gather.4.cloned.1.call-start = ((), (), s32[]{:S(2)}) async-start(), calls=%async_computation.4 | async-start | bytes 2367488 | tf_op jit(solution)/shard_map/all_gather | solution.py:68
  9.6 219.1 %reduce-scatter.2.cloned.1.call-start = ((), (), s32[]{:S(2)}) async-start(), calls=%async_computation.5 | async-start | bytes 4456448 | tf_op jit(solution)/shard_map/reduce_scatter | solution.py:118
  10.6 23.2 %collective-permute-start = (bf16[6,1536]{0,1:T(8,128)(2,1)S(1)}, bf16[6,1536]{0,1:T(8,128)(2,1)S(1)}, u32[]{:S(2)}, u32[]{:S(2)}) collective-permute-start(bf16[6,1536]{0,1:T(8,128)(2,1)S(1)} %bitcast.150), channel_id=1, source_target_pairs={{0,1},{1,2},{2,3},{3,4},{4,5},{5,6},{6,7},{7,8},{8,9},{9,10},{10,1... | collective-permute-start | bytes 55304 | tf_op jit(solution)/shard_map/ppermute | solution.py:17
  27.5 8.9 %collective-permute-start.6 = (bf16[2,128,256]{2,1,0:T(8,128)(2,1)S(1)}, bf16[2,128,256]{2,1,0:T(8,128)(2,1)S(1)}, u32[]{:S(2)}, u32[]{:S(2)}) collective-permute-start(bf16[2,128,256]{2,1,0:T(8,128)(2,1)S(1)} %dynamic-slice_bitcast_fusion.4), channel_id=1, source_target_pairs={{0,16},{16,0},{1,17},{17,1},{2,18},{18,2},{3,19},{19,3},{4,20},{20... | collective-permute-start | bytes 393224 | tf_op jit(solution)/shard_map/ppermute | solution.py:21
  34.2 1.0 copy-start.15
  34.5 0.8 copy-start.2
  43.5 16.2 %collective-permute-start.7 = (bf16[2,2,2,128,256]{4,3,2,1,0:T(8,128)(2,1)S(1)}, bf16[2,2,2,128,256]{4,3,2,1,0:T(8,128)(2,1)S(1)}, u32[]{:S(2)}, u32[]{:S(2)}) collective-permute-start(bf16[2,2,2,128,256]{4,3,2,1,0:T(8,128)(2,1)S(1)} %bitcast.136), channel_id=1, source_target_pairs={{0,32},{32,0},{1,33},{33,1},{2,34},{34,2},{3,35},{35,3},{4,36},{36... | collective-permute-start | bytes 1572872 | tf_op jit(solution)/shard_map/ppermute | solution.py:21
  45.5 13.0 %collective-permute-start.1 = (f32[127,512]{1,0:T(8,128)S(1)}, f32[127,512]{1,0:T(8,128)S(1)}, u32[]{:S(2)}, u32[]{:S(2)}) collective-permute-start(f32[127,512]{1,0:T(8,128)S(1)} %slice.71), channel_id=1, source_target_pairs={{0,1},{1,2},{2,3},{3,4},{4,5},{5,6},{6,7},{7,8},{8,9},{9,10},{10,1... | collective-permute-start | bytes 780296 | tf_op jit(solution)/shard_map/ppermute | solution.py:17
  99.6 10.4 %collective-permute-start.2 = (f32[64,512]{1,0:T(8,128)S(1)}, f32[64,512]{1,0:T(8,128)S(1)}, u32[]{:S(2)}, u32[]{:S(2)}) collective-permute-start(f32[64,512]{1,0:T(8,128)S(1)} %bitcast.153), channel_id=1, source_target_pairs={{0,16},{16,0},{1,17},{17,1},{2,18},{18,2},{3,19},{19,3},{4,20},{20... | collective-permute-start | bytes 393224 | tf_op jit(solution)/shard_map/ppermute | solution.py:21
  105.1 5.0 %copy-start.6 = (f32[2,128,512]{2,1,0:T(8,128)}, f32[2,128,512]{2,1,0:T(8,128)S(1)}, u32[]{:S(2)}) copy-start(f32[2,128,512]{2,1,0:T(8,128)S(1)} %fusion.1) | copy-start | bytes 1572868
  105.1 5.4 %copy-start.11 = (f32[1,255,512]{2,0,1:T(1,128)S(1)}, f32[1,255,512]{2,0,1:T(1,128)}, u32[]{:S(2)}) copy-start(f32[1,255,512]{2,0,1:T(1,128)} %broadcast_in_dim.34) | copy-start | bytes 1566724
  105.9 10.0 %collective-permute-start.8 = (f32[128,512]{1,0:T(8,128)}, f32[128,512]{1,0:T(8,128)S(1)}, u32[]{:S(2)}, u32[]{:S(2)}) collective-permute-start(f32[128,512]{1,0:T(8,128)} %dynamic-slice_bitcast_fusion.1), channel_id=1, source_target_pairs={{0,16},{16,0},{1,17},{17,1},{2,18},{18,2},{3,19},{19,3},{4,20},{20... | collective-permute-start | bytes 786440 | tf_op jit(solution)/shard_map/ppermute | solution.py:21
  110.5 5.3 %copy-start.7 = (f32[2,128,512]{2,1,0:T(8,128)S(1)}, f32[2,128,512]{2,1,0:T(8,128)}, u32[]{:S(2)}) copy-start(f32[2,128,512]{2,1,0:T(8,128)} %copy-done.6) | copy-start | bytes 1572868
  116.6 5.0 %copy-start.8 = (bf16[128,512]{1,0:T(8,128)(2,1)}, bf16[128,512]{1,0:T(8,128)(2,1)S(1)}, u32[]{:S(2)}) copy-start(bf16[128,512]{1,0:T(8,128)(2,1)S(1)} %get-tuple-element.28) | copy-start | bytes 393220
  116.7 8.5 %collective-permute-start.3 = (bf16[128,512]{1,0:T(8,128)(2,1)S(1)}, bf16[128,512]{1,0:T(8,128)(2,1)}, u32[]{:S(2)}, u32[]{:S(2)}) collective-permute-start(bf16[128,512]{1,0:T(8,128)(2,1)S(1)} %get-tuple-element.28), channel_id=1, source_target_pairs={{0,16},{16,0},{1,17},{17,1},{2,18},{18,2},{3,19},{19,3},{4,20},{20... | collective-permute-start | bytes 393224 | tf_op jit(solution)/shard_map/ppermute | solution.py:21
  126.1 2.8 %copy-start.4 = (bf16[1,128,512]{2,1,0:T(8,128)(2,1)}, bf16[1,128,512]{2,1,0:T(8,128)(2,1)S(1)}, u32[]{:S(2)}) copy-start(bf16[1,128,512]{2,1,0:T(8,128)(2,1)S(1)} %get-tuple-element.34) | copy-start | bytes 393220
  137.9 2.3 copy-start.5
  138.1 12.4 %collective-permute-start.9 = (f32[127,512]{1,0:T(8,128)}, f32[127,512]{1,0:T(8,128)S(1)}, u32[]{:S(2)}, u32[]{:S(2)}) collective-permute-start(f32[127,512]{1,0:T(8,128)} %bitcast.133), channel_id=1, source_target_pairs={{1,0},{2,1},{3,2},{4,3},{5,4},{6,5},{7,6},{8,7},{9,8},{10,9},{11,1... | collective-permute-start | bytes 780296 | tf_op jit(solution)/shard_map/ppermute | solution.py:17
  142.5 9.0 %copy-start.12 = (f32[128,1,512]{2,1,0:T(1,128)S(1)}, f32[128,1,512]{2,1,0:T(1,128)}, u32[]{:S(2)}) copy-start(f32[128,1,512]{2,1,0:T(1,128)} %broadcast_in_dim_reshape.6) | copy-start | bytes 786436
  143.7 33.5 %collective-permute-start.4 = (f32[2,2,2,128,256]{4,3,2,1,0:T(8,128)}, f32[2,2,2,128,256]{4,3,2,1,0:T(8,128)}, u32[]{:S(2)}, u32[]{:S(2)}) collective-permute-start(f32[2,2,2,128,256]{4,3,2,1,0:T(8,128)} %dynamic-slice_bitcast_fusion), channel_id=1, source_target_pairs={{0,32},{32,0},{1,33},{33,1},{2,34},{34,2},{3,35},{35,3},{4,36},{36... | collective-permute-start | bytes 3145736 | tf_op jit(solution)/shard_map/ppermute | solution.py:21
  154.4 1.1 copy-start.3
  154.5 2.7 %copy-start = (f32[128,512]{1,0:T(8,128)}, f32[128,512]{1,0:T(8,128)S(1)}, u32[]{:S(2)}) copy-start(f32[128,512]{1,0:T(8,128)S(1)} %get-tuple-element.21) | copy-start | bytes 786436
  155.5 2.1 copy-start.9
  155.5 12.0 %copy-start.10 = (f32[16,4,512]{2,1,0:T(4,128)S(1)}, f32[16,4,512]{2,1,0:T(4,128)}, u32[]{:S(2)}) copy-start(f32[16,4,512]{2,1,0:T(4,128)} %get-tuple-element.31) | copy-start | bytes 393220
  157.7 9.8 %collective-permute-start.11 = (f32[16,6,512]{2,1,0:T(8,128)S(1)}, f32[16,6,512]{2,1,0:T(8,128)S(1)}, u32[]{:S(2)}, u32[]{:S(2)}) collective-permute-start(f32[16,6,512]{2,1,0:T(8,128)S(1)} %pad_maximum_fusion.3), channel_id=1, source_target_pairs={{0,16},{16,0},{1,17},{17,1},{2,18},{18,2},{3,19},{19,3},{4,20},{20... | collective-permute-start | bytes 589832 | tf_op jit(solution)/shard_map/ppermute | solution.py:21
  168.2 28.9 %all-to-all-start.1 = ((f32[16,6,512]{2,1,0:T(8,128)}), f32[16,6,512]{2,1,0:T(8,128)S(1)}, u32[]{:S(2)}, u32[]{:S(2)}) async-start(f32[16,6,512]{2,1,0:T(8,128)} %fusion.24), calls=%async_computation.1 | async-start | bytes 524288 | tf_op jit(solution)/shard_map/all_to_all | solution.py:138
  177.2 37.9 %copy-start.1 = (f32[128,512]{1,0:T(8,128)S(1)}, f32[128,512]{1,0:T(8,128)}, u32[]{:S(2)}) copy-start(f32[128,512]{1,0:T(8,128)} %copy-done) | copy-start | bytes 786436
  197.1 12.2 %all-to-all-start = ((bf16[8,128,256]{2,1,0:T(8,128)(2,1)}), bf16[8,128,256]{2,1,0:T(8,128)(2,1)S(1)}, u32[]{:S(2)}, u32[]{:S(2)}) async-start(bf16[8,128,256]{2,1,0:T(8,128)(2,1)} %bitcast.22), calls=%async_computation | async-start | bytes 1048576 | tf_op jit(solution)/shard_map/all_to_all | solution.py:113
  204.1 10.9 %collective-permute-start.10 = (f32[6,1536]{1,0:T(8,128)S(1)}, f32[6,1536]{1,0:T(8,128)S(1)}, u32[]{:S(2)}, u32[]{:S(2)}) collective-permute-start(f32[6,1536]{1,0:T(8,128)S(1)} %slice.77), channel_id=1, source_target_pairs={{1,0},{2,1},{3,2},{4,3},{5,4},{6,5},{7,6},{8,7},{9,8},{10,9},{11,1... | collective-permute-start | bytes 110600 | tf_op jit(solution)/shard_map/ppermute | solution.py:17
  210.0 17.9 %all-to-all-start.2 = ((f32[16,2,512]{2,1,0:T(2,128)}), f32[16,2,512]{2,1,0:T(2,128)S(1)}, u32[]{:S(2)}, u32[]{:S(2)}) async-start(f32[16,2,512]{2,1,0:T(2,128)} %broadcast_in_dim.40), calls=%async_computation.2 | async-start | bytes 131072 | tf_op jit(solution)/shard_map/all_to_all | solution.py:141
  215.2 7.1 %copy-start.14 = (f32[3,7,512]{2,1,0:T(8,128)S(1)}, f32[3,7,512]{2,1,0:T(8,128)}, u32[]{:S(2)}) copy-start(f32[3,7,512]{2,1,0:T(8,128)} %param.6) | copy-start | bytes 129028
  216.4 12.2 %collective-permute-start.5 = (bf16[128,256]{1,0:T(8,128)(2,1)S(1)}, bf16[128,256]{1,0:T(8,128)(2,1)S(1)}, u32[]{:S(2)}, u32[]{:S(2)}) collective-permute-start(bf16[128,256]{1,0:T(8,128)(2,1)S(1)} %reduce_sum.21), channel_id=1, source_target_pairs={{0,0},{1,1},{2,2},{3,3},{4,4},{5,5},{6,6},{7,7},{8,8},{9,9},{10,10... | collective-permute-start | bytes 196616 | tf_op jit(solution)/shard_map/ppermute | solution.py:115
Sparse Core Ops, SparseCore 0:
  10.6 87.9 all-gather.3
  129.0 83.9 reduce-scatter.1

commit v2 on v1

v2 whole, which is shorter than its diff:
```python
import jax
import jax.numpy as jnp
from jax import lax
from jax.experimental import pallas as pl
from jax.experimental.pallas import tpu as pltpu
from jax.sharding import Mesh, PartitionSpec as P

F32 = jnp.float32
BF16 = jnp.bfloat16
AXES = ("x", "yl", "co", "yh", "zh", "zl")
SIZES = (4, 2, 2, 2, 8, 2)
ALONG = ("zh", "zl")
CTX = ("yh", "zh", "zl")
FSDP = ("x", "yl", "co")
ROWS = 128
CHANNELS = 512
WIDE = 128
ZS = 16


def passed_along(value, steps):
    count = 32
    first, last = (max(0, -steps), min(count, count - steps))
    return lax.ppermute(value, CTX, [(source, source + steps) for source in range(first, last)])


def swapped(value, axis):
    return lax.ppermute(value, axis, [(0, 1), (1, 0)])


def ordered(index, own, other):
    first = jnp.where(index == 0, own, other)
    second = jnp.where(index == 0, other, own)
    return jnp.stack([first, second])


def after(value, *others):
    return lax.optimization_barrier((value, *others))[0]


def depthwise(padded, kernel):
    result = lax.conv_general_dilated(
        padded[None],
        kernel[:, None, :],
        (1,),
        "VALID",
        dimension_numbers=("NWC", "WIO", "NWC"),
        feature_group_count=padded.shape[1],
        precision=lax.Precision.HIGHEST,
    )
    return result[0]


def owner_pairs():
    pairs = []
    for x in range(4):
        for rest in range(4):
            for yh in range(2):
                for z in range(16):
                    source = ((x * 4 + rest) * 2 + yh) * 16 + z
                    target = (((2 * yh + x % 2) * 4 + rest) * 2 + x // 2) * 16 + z
                    pairs.append((source, target))
    return pairs


def gated_grad_kernel(yh_ref, grads_ref, proj_ref, kept_ref, given_ref):
    yh = yh_ref[0]

    def rows_of(block):
        total = jnp.zeros((ROWS, CHANNELS), F32)
        for z in range(ZS):
            total += lax.dot_general(
                grads_ref[z, pl.ds(pl.multiple_of(block * ROWS, ROWS), ROWS), :],
                proj_ref[z, :CHANNELS, :],
                (((1,), (1,)), ((), ())),
                preferred_element_type=F32,
            )
        return total

    given_ref[...] = rows_of(1 - yh).astype(BF16)
    kept_ref[...] = rows_of(yh)


def layer_out_kernel(gated_ref, proj_ref, out_ref):
    for z in range(ZS):
        terms = jnp.dot(gated_ref[...], proj_ref[z], preferred_element_type=F32).astype(BF16)
        columns = pl.ds((z % 2) * WIDE, WIDE)
        out_ref[z // 2, :, columns] = terms[:ROWS]
        out_ref[ZS // 2 + z // 2, :, columns] = terms[ROWS:]


def grad_proj_kernel(gated_ref, grads_ref, out_ref):
    for z in range(ZS):
        out_ref[z] = lax.dot_general(
            gated_ref[...], grads_ref[z], (((0,), (0,)), ((), ())), preferred_element_type=F32
        )


def call(kernel, outs, flops, args):
    specs = [
        pl.BlockSpec(memory_space=pltpu.SMEM if arg.ndim == 1 else pltpu.VMEM) for arg in args
    ]
    size = sum(arg.size * arg.dtype.itemsize for arg in args)
    size += sum(out.size * out.dtype.itemsize for out in outs)
    return pl.pallas_call(
        kernel,
        out_shape=outs,
        in_specs=specs,
        out_specs=[pl.BlockSpec(memory_space=pltpu.VMEM) for _ in outs],
        cost_estimate=pl.CostEstimate(flops=flops, bytes_accessed=size, transcendentals=0),
        compiler_params=pltpu.CompilerParams(vmem_limit_bytes=32 * 1024 * 1024),
    )(*args)


def shaped(shape, dtype):
    return jax.ShapeDtypeStruct(shape, dtype)


MATMUL = 2 * 256 * 512 * 2048


def local(qkv, short_filter, long_filter, proj, out_grad):
    rows = qkv.shape[0]
    channels = qkv.shape[2]
    reach_short = short_filter.shape[1]
    taps_here = long_filter.shape[0]
    yh = lax.axis_index("yh")
    co = lax.axis_index("co")

    gathered = lax.all_gather(proj, ALONG, axis=0, tiled=False)

    taps_pair = ordered(yh, long_filter, swapped(long_filter, "yh"))
    taps_copies = jnp.broadcast_to(taps_pair[None], (ZS,) + taps_pair.shape)
    taps_all = lax.all_to_all(taps_copies, ALONG, 0, 0, tiled=True)
    long_taps = jnp.transpose(taps_all, (1, 0, 2, 3)).reshape(2 * ZS * taps_here, channels)
    reach_long = long_taps.shape[0]

    copies = after(jnp.broadcast_to(out_grad[None], (ZS,) + out_grad.shape), taps_all)
    blocks = lax.all_to_all(copies, ("x", "yl", "yh"), 0, 0, tiled=True)
    blocks = blocks.reshape(2, 8, rows, 2 * WIDE)
    half = lax.dynamic_index_in_dim(blocks, yh, 0, keepdims=False)
    both = ordered(co, half, swapped(half, "co")).reshape(2, 2, 2, 2, rows, 2, WIDE)
    grads = jnp.transpose(both, (1, 2, 0, 5, 3, 4, 6)).reshape(ZS, 2 * rows, WIDE)

    inputs = qkv.reshape(rows, 3 * channels)
    reach = reach_short - 1
    sent = jnp.concatenate([inputs[:, channels:], inputs[rows - 8 :, :channels].reshape(4, 2 * channels)], axis=0)
    before = passed_along(sent, 1)
    far = passed_along(inputs[rows - 8 :, channels:], 2)
    query_rim = before[rows:].reshape(8, channels)[8 - reach :]
    before = before[:rows]
    rim = jnp.concatenate([query_rim, before[rows - reach :]], axis=1)
    extended = jnp.concatenate([rim, inputs], axis=0).astype(F32)
    short_taps = jnp.transpose(short_filter, (1, 0, 2)).reshape(reach_short, 3 * channels)
    query_side = depthwise(extended[:, :channels], short_taps[::-1, :channels])
    pairs = jnp.concatenate([far[8 - reach :], before, inputs[:, channels:]], axis=0)
    pairs = depthwise(pairs.astype(F32), short_taps[::-1, channels:])
    key_side = pairs[rows:, :channels]
    value_side = pairs[rows:, channels:]
    product_ext = (pairs[:, :channels] * pairs[:, channels:])[2 * rows - (rows + reach_long - 1) :]

    long_mix = depthwise(product_ext, long_taps[::-1])
    gated_out = (query_side * long_mix).astype(BF16)
    gated_both = ordered(yh, gated_out, swapped(gated_out, "yh")).reshape(2 * rows, channels)

    (proj_part,) = call(
        grad_proj_kernel, [shaped((ZS, channels, WIDE), F32)], MATMUL, [gated_both, grads]
    )
    grad_proj = lax.psum_scatter(
        proj_part.reshape(ZS * channels, WIDE), ALONG, scatter_dimension=0, tiled=True
    )

    gathered = after(gathered, proj_part)

    part_kept, part_given = call(
        gated_grad_kernel,
        [shaped((rows, channels), F32), shaped((rows, channels), BF16)],
        MATMUL,
        [yh.reshape(1), grads, gathered],
    )
    gated_grad = part_kept + swapped(part_given, "yh").astype(F32)

    (out_part,) = call(
        layer_out_kernel,
        [shaped((ZS, rows, 2 * WIDE), BF16)],
        MATMUL,
        [after(gated_both, proj_part), gathered],
    )
    out_terms = lax.all_to_all(out_part, FSDP, 0, 0, tiled=True)

    query_grad = gated_grad * long_mix
    mixed_grad = gated_grad * query_side
    mixed_rim = passed_along(mixed_grad.astype(BF16), -1).astype(F32)[: reach_long - 1]
    long_part = depthwise(product_ext, mixed_grad)[::-1].reshape(2, ZS, taps_here, channels)
    mixed_ext = jnp.concatenate([mixed_grad, after(mixed_rim, out_part, long_part)], axis=0)
    product_grad = depthwise(mixed_ext, long_taps)
    short_grad = jnp.concatenate([query_grad, product_grad * value_side, product_grad * key_side], axis=1)
    short_rim = passed_along(short_grad[: reach_short - 1], -1)
    grad_inputs = depthwise(jnp.concatenate([short_grad, short_rim], axis=0), short_taps)
    grad_qkv = grad_inputs.reshape(rows, 3, channels).astype(BF16)
    short_part = depthwise(extended, short_grad)[::-1]

    short_rows = jnp.pad(short_part.reshape(3 * reach_short, channels), ((0, 3), (0, 0)))
    long_kept = lax.dynamic_index_in_dim(long_part, yh, 0, keepdims=False)
    long_given = lax.dynamic_index_in_dim(long_part, 1 - yh, 0, keepdims=False)
    terms_given = jnp.concatenate([long_given.reshape(ZS * taps_here, channels), short_rows], axis=0)
    terms_got = swapped(terms_given, "yh")
    long_half = long_kept + terms_got[: ZS * taps_here].reshape(long_kept.shape)
    short_pair = (short_rows + terms_got[ZS * taps_here :]).astype(BF16)
    short_pair, out_terms, long_half = lax.optimization_barrier((short_pair, out_terms, long_half))
    grad_long = jnp.sum(lax.all_to_all(long_half, ALONG, 0, 0, tiled=True), axis=0)

    out_sum = jnp.sum(out_terms.astype(F32), axis=0).astype(BF16)
    layer_out = lax.ppermute(out_sum, AXES, owner_pairs())

    short_sum = jnp.sum(lax.all_gather(short_pair, ALONG, axis=0, tiled=False).astype(F32), axis=0)
    grad_short = jnp.transpose(short_sum[: 3 * reach_short].reshape(reach_short, 3, channels), (1, 0, 2))
    return (layer_out, grad_qkv, grad_short, grad_long, grad_proj)


def solution(mesh):
    fine = Mesh(mesh.devices.reshape(SIZES), AXES)
    in_specs = (
        P(CTX, None, FSDP),
        P(None, None, FSDP),
        P(CTX, FSDP),
        P(FSDP, CTX),
        P(CTX, FSDP),
    )
    out_specs = (
        P(CTX, FSDP),
        P(CTX, None, FSDP),
        P(None, None, FSDP),
        P(CTX, FSDP),
        P(FSDP, CTX),
    )
    return jax.shard_map(local, mesh=fine, in_specs=in_specs, out_specs=out_specs, check_vma=False)
```

time: 239 us -> 211 us (0.88)
  waiting for transfers between devices: 85.3 us -> 41.9 us
  blocking collectives: 20 us -> 32.2 us
  starting transfers between devices: 61.7 us -> 72.9 us
  matrix products: 20.1 us -> 14.8 us
  Pallas kernels: 0 us -> 4.8 us
  other arithmetic: 10 us -> 6.03 us
    all_gather x1, waiting for transfers between devices: 36.8 us -> 0.49 us  [local(): gathered = lax.all_gather(proj, ALONG, axis=0, tiled=False)]
    all_gather x2 -> x1, blocking collectives: 20 us -> 32.2 us  [local(): lax.all_gather(short_pair, ALONG, axis=0, tiled=False).astype(F32)]
    ppermute x4, waiting for transfers between devices: 13.9 us -> 4.79 us  [passed_along(): lax.ppermute(value, CTX, [(source, source + steps) for source in range(fi...]
    dot_general x3 -> x0, matrix products: 7.38 us -> none  [the longest x1 2.71 us: local(): lax.dot_general(gated_both, grads, (((0,), (0,)), ((), ())), preferred_el...]
    all_to_all x3 -> x4, starting transfers between devices: 20.2 us -> 26.9 us  [the longest x1 12.5 us: local(): taps_all = lax.all_to_all(taps_copies, ALONG, 0, 0, tiled=True)]
    dot_general x3 -> x0, local copies, waits for them, and re-layouts: 5.12 us -> none  [the longest x2 4.3 us: local(): out_part = jnp.dot(gated_both, proj_half, preferred_element_type=F32)]
    pallas_call x0 -> x3, Pallas kernels: none -> 4.8 us  [call(): pl.pallas_call(kernel, out_shape=outs, in_specs=specs, out_specs=[pl.Bloc...]
    all_to_all x3 -> x4, waiting for transfers between devices: 24.6 us -> 28.3 us  [the longest x1 25 us: local(): taps_all = lax.all_to_all(taps_copies, ALONG, 0, 0, tiled=True)]
  transfers between devices with their start and end apart: 17 -> 16, of which waited for: 9 -> 6; matrix products, arithmetic and copies ran while one was open for 19% -> 18% of each run, Pallas kernels for 0% -> 2%
where the time goes in v2:
time: 211 us; the launch traced here: 210 us
  starting transfers between devices  72.9 us (35%)
  waiting for transfers between devices  41.9 us (20%)
  blocking collectives  32.2 us (15%)
  local copies, waits for them, and re-layouts  22 us (10%)
  between operations  14.9 us (7%)
  matrix products  14.8 us (7%)
  other arithmetic  6.03 us (3%)
  Pallas kernels  4.8 us (2%)
    all_gather x1, blocking collectives, local(): lax.all_gather(short_pair, ALONG, axis=0, tiled=False).astype(F32)  32.2 us
    ppermute x5, starting transfers between devices, swapped(): return lax.ppermute(value, axis, [(0, 1), (1, 0)])  28.3 us
    all_to_all x1, waiting for transfers between devices, local(): taps_all = lax.all_to_all(taps_copies, ALONG, 0, 0, tiled=True)  25 us
    conv_general_dilated x7, matrix products, depthwise(): lax.conv_general_dilated(padded[None], kernel[:, None, :], (1,), 'VALID',...  14.8 us
    all_to_all x1, starting transfers between devices, local(): taps_all = lax.all_to_all(taps_copies, ALONG, 0, 0, tiled=True)  12.5 us
    ppermute x4, starting transfers between devices, passed_along(): lax.ppermute(value, CTX, [(source, source + steps) for source in range(fi...  11.9 us
    ppermute x5, waiting for transfers between devices, swapped(): return lax.ppermute(value, axis, [(0, 1), (1, 0)])  8.29 us
    unnamed x46, local copies, waits for them, and re-layouts  8.02 us
  transfers between devices with their start and end apart: 16, of which 6 were waited for; matrix products, arithmetic and copies ran while one was open for 18% of the time, Pallas kernels for 2%

profile of v2, /device:TPU:6, one launch (start us, length us, event | category | flops | bytes accessed | tf_op | source)
XLA Modules:
  0.0 209.6 jit_solution(9254020854255071805)
XLA Ops:
  7.2 5.1 %collective-permute-start.1 = (f32[4,512]{1,0:T(4,128)}, f32[4,512]{1,0:T(4,128)S(1)}, u32[]{:S(2)}, u32[]{:S(2)}) collective-permute-start(f32[4,512]{1,0:T(4,128)} %param.7), channel_id=1, source_target_pairs={{0,16},{16,0},{1,17},{17,1},{2,18},{18,2},{3,19},{19,3},{4,20},{20... | collective-permute-start | bytes 24584 | tf_op jit(solution)/shard_map/ppermute | solution.py:28
  12.3 1.2 copy.148
  14.1 3.9 %collective-permute-start = (bf16[132,1024]{0,1:T(8,128)(2,1)S(1)}, bf16[132,1024]{0,1:T(8,128)(2,1)S(1)}, u32[]{:S(2)}, u32[]{:S(2)}) collective-permute-start(bf16[132,1024]{0,1:T(8,128)(2,1)S(1)} %pad_maximum_fusion.2), channel_id=1, source_target_pairs={{0,1},{1,2},{2,3},{3,4},{4,5},{5,6},{6,7},{7,8},{8,9},{9,10},{10,1... | collective-permute-start | bytes 811016 | tf_op jit(solution)/shard_map/ppermute | solution.py:24
  18.1 5.2 %collective-permute-start.3 = (bf16[8,1024]{0,1:T(8,128)(2,1)S(1)}, bf16[8,1024]{0,1:T(8,128)(2,1)S(1)}, u32[]{:S(2)}, u32[]{:S(2)}) collective-permute-start(bf16[8,1024]{0,1:T(8,128)(2,1)S(1)} %slice.100), channel_id=1, source_target_pairs={{0,2},{1,3},{2,4},{3,5},{4,6},{5,7},{6,8},{7,9},{8,10},{9,11},{10,... | collective-permute-start | bytes 49160 | tf_op jit(solution)/shard_map/ppermute | solution.py:24
  23.8 0.7 copy.154
  24.5 0.8 broadcast_in_dim.48
  25.3 12.5 %all-to-all-start = ((f32[16,2,4,512]{3,2,1,0:T(4,128)}), f32[16,2,4,512]{3,2,1,0:T(4,128)}, u32[]{:S(2)}, u32[]{:S(2)}) async-start(f32[16,2,4,512]{3,2,1,0:T(4,128)} %broadcast_in_dim.48), calls=%async_computation | async-start | bytes 524288 | tf_op jit(solution)/shard_map/all_to_all | solution.py:134
  38.4 1.2 copy.160
  39.6 2.2 %fusion.30 = f32[1,256,1024]{2,0,1:T(1,128)S(1)} fusion(bf16[1,262,1024]{2,0,1:T(2,128)(2,1)S(1)} %copy.160, f32[7,1,1024]{2,1,0:T(1,128)S(1)} %broadcast_in_dim.52), kind=kOutput, calls=%fused_computation.65 | convolution fusion | flops 22020096 | bytes 1613824 | tf_op jit(solution)/shard_map/conv_general_dilated | solution.py:42
  43.4 25.0 %all-to-all-done = f32[16,2,4,512]{3,2,1,0:T(4,128)} async-done(((f32[16,2,4,512]{3,2,1,0:T(4,128)}), f32[16,2,4,512]{3,2,1,0:T(4,128)}, u32[]{:S(2)}, u32[]{:S(2)}) %all-to-all-start) | async-done | bytes 262176 | tf_op jit(solution)/shard_map/all_to_all | solution.py:134
  68.5 1.2 broadcast_in_dim.47
  69.6 5.1 %all-to-all-start.1 = ((bf16[16,128,256]{1,2,0:T(8,128)(2,1)}), bf16[16,128,256]{1,2,0:T(8,128)(2,1)S(1)}, u32[]{:S(2)}, u32[]{:S(2)}) async-start(bf16[16,128,256]{1,2,0:T(8,128)(2,1)} %broadcast_in_dim.47), calls=%async_computation.1 | async-start | bytes 2097152 | tf_op jit(solution)/shard_map/all_to_all | solution.py:139
  75.3 1.0 fusion.9
  76.3 1.0 copy.161
  77.4 1.3 rev.17
  78.8 3.8 %fusion.14 = f32[1,128,512]{2,0,1:T(1,128)S(1)} fusion(f32[1,255,512]{2,1,0:T(8,128)S(1)} %copy-done.11, f32[128,1,512]{2,0,1:T(8,128)} %bitcast.103), kind=kOutput, calls=%fused_computation.29 | convolution fusion | flops 100663296 | bytes 1046528 | tf_op jit(solution)/shard_map/conv_general_dilated | solution.py:42
  82.6 3.3 %all-to-all-done.1 = bf16[16,128,256]{1,2,0:T(8,128)(2,1)S(1)} async-done(((bf16[16,128,256]{1,2,0:T(8,128)(2,1)}), bf16[16,128,256]{1,2,0:T(8,128)(2,1)S(1)}, u32[]{:S(2)}, u32[]{:S(2)}) %all-to-all-start.1) | async-done | bytes 1048608 | tf_op jit(solution)/shard_map/all_to_all | solution.py:139
  85.9 1.9 collective-permute-start.2
  87.9 3.3 %collective-permute-start.4 = (bf16[128,512]{1,0:T(8,128)(2,1)S(1)}, bf16[128,512]{1,0:T(8,128)(2,1)S(1)}, u32[]{:S(2)}, u32[]{:S(2)}) collective-permute-start(bf16[128,512]{1,0:T(8,128)(2,1)S(1)} %fusion.16), channel_id=1, source_target_pairs={{0,16},{16,0},{1,17},{17,1},{2,18},{18,2},{3,19},{19,3},{4,20},{20... | collective-permute-start | bytes 393224 | tf_op jit(solution)/shard_map/ppermute | solution.py:28
  91.2 6.0 %collective-permute-done.4 = bf16[128,512]{1,0:T(8,128)(2,1)S(1)} collective-permute-done((bf16[128,512]{1,0:T(8,128)(2,1)S(1)}, bf16[128,512]{1,0:T(8,128)(2,1)S(1)}, u32[]{:S(2)}, u32[]{:S(2)}) %collective-permute-start.4) | collective-permute-done | bytes 131104 | tf_op jit(solution)/shard_map/ppermute | solution.py:28
  97.3 1.1 broadcast_select_fusion.1
  98.5 0.7 copy.155
  99.2 1.3 shard_map.92
  100.5 2.0 copy-done
  103.0 1.6 copy-done.1
  104.6 1.2 shard_map.93
  105.9 4.1 %collective-permute-start.5 = (bf16[128,512]{1,0:T(8,128)(2,1)S(1)}, bf16[128,512]{1,0:T(8,128)(2,1)}, u32[]{:S(2)}, u32[]{:S(2)}) collective-permute-start(bf16[128,512]{1,0:T(8,128)(2,1)S(1)} %get-tuple-element.17), channel_id=1, source_target_pairs={{0,16},{16,0},{1,17},{17,1},{2,18},{18,2},{3,19},{19,3},{4,20},{20... | collective-permute-start | bytes 393224 | tf_op jit(solution)/shard_map/ppermute | solution.py:28
  109.9 2.0 copy.168
  112.0 1.3 broadcast_in_dim_reshape.6
  113.3 2.3 %shard_map.94 = bf16[16,128,256]{2,1,0:T(8,128)(2,1)} custom-call(bf16[256,512]{1,0:T(8,128)(2,1)S(1)} %bitcast.88, bf16[16,512,128]{2,1,0:T(8,128)(2,1)S(1)} %bitcast.86), custom_call_target="tpu_custom_call" | custom-call | flops 536870912 | bytes 3407872 | tf_op jit(solution)/shard_map/pallas_call | solution.py:105
  115.5 5.7 %all-to-all-start.2 = ((bf16[16,128,256]{2,1,0:T(8,128)(2,1)}), bf16[16,128,256]{2,1,0:T(8,128)(2,1)S(1)}, u32[]{:S(2)}, u32[]{:S(2)}) async-start(bf16[16,128,256]{2,1,0:T(8,128)(2,1)} %shard_map.94), calls=%async_computation.2 | async-start | bytes 2097152 | tf_op jit(solution)/shard_map/all_to_all | solution.py:189
  121.2 1.0 fusion.28
  122.3 1.5 collective-permute-start.6
  123.7 2.9 %fusion.12 = f32[1,128,512]{2,0,1:T(1,128)S(1)} fusion(f32[1,255,512]{2,1,0:T(8,128)S(1)} %copy-done.12, f32[128,1,512]{2,0,1:T(8,128)S(1)} %bitcast.102), kind=kOutput, calls=%fused_computation.27 | convolution fusion | flops 100663296 | bytes 1046528 | tf_op jit(solution)/shard_map/conv_general_dilated | solution.py:42
  127.0 4.8 %collective-permute-done.6 = bf16[128,512]{1,0:T(8,128)(2,1)S(1)} collective-permute-done((bf16[128,512]{1,0:T(8,128)(2,1)S(1)}, bf16[128,512]{1,0:T(8,128)(2,1)S(1)}, u32[]{:S(2)}, u32[]{:S(2)}) %collective-permute-start.6) | collective-permute-done | bytes 131104 | tf_op jit(solution)/shard_map/ppermute | solution.py:24
  131.8 2.8 %fusion.10 = f32[1,128,512]{2,0,1:T(1,128)S(1)} fusion(f32[128,1,512]{2,1,0:T(1,128)S(1)} %broadcast_in_dim_reshape.6, f32[1,255,512]{2,1,0:T(8,128)S(1)} %maximum_bitcast_fusion.3), kind=kOutput, calls=%fused_computation.25 | convolution fusion | flops 100663296 | bytes 1046528 | tf_op jit(solution)/shard_map/conv_general_dilated | solution.py:42
  134.9 1.4 collective-permute-start.9
  136.3 2.1 %fusion.5 = f32[1,7,1536]{2,0,1:T(1,128)S(1)} fusion(bf16[1,134,1536]{2,0,1:T(2,128)(2,1)S(1)} %copy-done.10, f32[128,1,1536]{2,0,1:T(8,128)S(1)} %get-tuple-element.62), kind=kOutput, calls=%fused_computation.14 | convolution fusion | flops 16515072 | bytes 1241088 | tf_op jit(solution)/shard_map/conv_general_dilated | solution.py:42
  138.8 14.0 %collective-permute-start.7 = (f32[88,512]{1,0:T(8,128)S(1)}, f32[88,512]{1,0:T(8,128)S(1)}, u32[]{:S(2)}, u32[]{:S(2)}) collective-permute-start(f32[88,512]{1,0:T(8,128)S(1)} %pad_maximum_fusion.4), channel_id=1, source_target_pairs={{0,16},{16,0},{1,17},{17,1},{2,18},{18,2},{3,19},{19,3},{4,20},{20... | collective-permute-start | bytes 540680 | tf_op jit(solution)/shard_map/ppermute | solution.py:28
  153.0 1.0 reshape.79
  154.1 2.3 %collective-permute-done.7 = f32[88,512]{1,0:T(8,128)S(1)} collective-permute-done((f32[88,512]{1,0:T(8,128)S(1)}, f32[88,512]{1,0:T(8,128)S(1)}, u32[]{:S(2)}, u32[]{:S(2)}) %collective-permute-start.7) | collective-permute-done | bytes 180256 | tf_op jit(solution)/shard_map/ppermute | solution.py:28
  156.4 0.7 bitcast_add_fusion
  157.1 3.6 %all-to-all-start.3 = ((f32[16,4,512]{2,1,0:T(4,128)}), f32[16,4,512]{2,1,0:T(4,128)S(1)}, u32[]{:S(2)}, u32[]{:S(2)}) async-start(f32[16,4,512]{2,1,0:T(4,128)} %bitcast_add_fusion), calls=%async_computation.3 | async-start | bytes 262144 | tf_op jit(solution)/shard_map/all_to_all | solution.py:211
  161.8 0.9 copy.175
  162.8 5.7 %collective-permute-start.8 = (bf16[128,256]{1,0:T(8,128)(2,1)S(1)}, bf16[128,256]{1,0:T(8,128)(2,1)S(1)}, u32[]{:S(2)}, u32[]{:S(2)}) collective-permute-start(bf16[128,256]{1,0:T(8,128)(2,1)S(1)} %reduce_sum.30), channel_id=1, source_target_pairs={{0,0},{1,1},{2,2},{3,3},{4,4},{5,5},{6,6},{7,7},{8,8},{9,9},{10,10... | collective-permute-start | bytes 196616 | tf_op jit(solution)/shard_map/ppermute | solution.py:214
  168.5 32.2 %all-gather.1 = bf16[384,512]{1,0:T(8,128)(2,1)S(1)} all-gather(bf16[24,512]{1,0:T(8,128)(2,1)S(1)} %fusion.19), channel_id=3, replica_groups=mesh['x'=4,'yl'=2,'co'=2,'yh'=2,'zh'=8,'zl'=2] {'zh','zl'}, dimensions={0}, use_global_device_ids=true | all-gather | bytes 417792 | tf_op jit(solution)/shard_map/all_gather | solution.py:216
  200.8 0.6 copy.176
  201.5 0.6 reduce_sum.32
  (116 shorter events, 7.6 us)
Async XLA Ops:
  7.2 95.8 %all-gather.4.cloned.1.call-start = ((), (), s32[]{:S(2)}) async-start(), calls=%async_computation.6 | async-start | bytes 2228224 | tf_op jit(solution)/shard_map/all_gather | solution.py:130
  7.2 17.3 %collective-permute-start.1 = (f32[4,512]{1,0:T(4,128)}, f32[4,512]{1,0:T(4,128)S(1)}, u32[]{:S(2)}, u32[]{:S(2)}) collective-permute-start(f32[4,512]{1,0:T(4,128)} %param.7), channel_id=1, source_target_pairs={{0,16},{16,0},{1,17},{17,1},{2,18},{18,2},{3,19},{19,3},{4,20},{20... | collective-permute-start | bytes 24584 | tf_op jit(solution)/shard_map/ppermute | solution.py:28
  13.5 9.8 %copy-start.15 = (f32[3,7,512]{2,1,0:T(8,128)S(1)}, f32[3,7,512]{2,1,0:T(8,128)}, u32[]{:S(2)}) copy-start(f32[3,7,512]{2,1,0:T(8,128)} %param.6) | copy-start | bytes 129028
  13.6 10.2 %copy-start.14 = (bf16[128,256]{1,0:T(8,128)(2,1)S(1)}, bf16[128,256]{1,0:T(8,128)(2,1)}, u32[]{:S(2)}) copy-start(bf16[128,256]{1,0:T(8,128)(2,1)} %param.9) | copy-start | bytes 196612
  13.6 10.9 %copy-start.17 = (f32[4,512]{1,0:T(4,128)S(1)}, f32[4,512]{1,0:T(4,128)}, u32[]{:S(2)}) copy-start(f32[4,512]{1,0:T(4,128)} %param.7) | copy-start | bytes 24580
  14.1 23.9 %collective-permute-start = (bf16[132,1024]{0,1:T(8,128)(2,1)S(1)}, bf16[132,1024]{0,1:T(8,128)(2,1)S(1)}, u32[]{:S(2)}, u32[]{:S(2)}) collective-permute-start(bf16[132,1024]{0,1:T(8,128)(2,1)S(1)} %pad_maximum_fusion.2), channel_id=1, source_target_pairs={{0,1},{1,2},{2,3},{3,4},{4,5},{5,6},{6,7},{7,8},{8,9},{9,10},{10,1... | collective-permute-start | bytes 811016 | tf_op jit(solution)/shard_map/ppermute | solution.py:24
  18.1 19.7 %collective-permute-start.3 = (bf16[8,1024]{0,1:T(8,128)(2,1)S(1)}, bf16[8,1024]{0,1:T(8,128)(2,1)S(1)}, u32[]{:S(2)}, u32[]{:S(2)}) collective-permute-start(bf16[8,1024]{0,1:T(8,128)(2,1)S(1)} %slice.100), channel_id=1, source_target_pairs={{0,2},{1,3},{2,4},{3,5},{4,6},{5,7},{6,8},{7,9},{8,10},{9,11},{10,... | collective-permute-start | bytes 49160 | tf_op jit(solution)/shard_map/ppermute | solution.py:24
  25.3 43.2 %all-to-all-start = ((f32[16,2,4,512]{3,2,1,0:T(4,128)}), f32[16,2,4,512]{3,2,1,0:T(4,128)}, u32[]{:S(2)}, u32[]{:S(2)}) async-start(f32[16,2,4,512]{3,2,1,0:T(4,128)} %broadcast_in_dim.48), calls=%async_computation | async-start | bytes 524288 | tf_op jit(solution)/shard_map/all_to_all | solution.py:134
  42.0 1.3 copy-start.3
  43.1 25.4 %copy-start.13 = (bf16[128,256]{0,1:T(8,128)(2,1)S(1)}, bf16[128,256]{0,1:T(8,128)(2,1)}, u32[]{:S(2)}) copy-start(bf16[128,256]{0,1:T(8,128)(2,1)} %copy.154) | copy-start | bytes 196612
  69.6 16.3 %all-to-all-start.1 = ((bf16[16,128,256]{1,2,0:T(8,128)(2,1)}), bf16[16,128,256]{1,2,0:T(8,128)(2,1)S(1)}, u32[]{:S(2)}, u32[]{:S(2)}) async-start(bf16[16,128,256]{1,2,0:T(8,128)(2,1)} %broadcast_in_dim.47), calls=%async_computation.1 | async-start | bytes 2097152 | tf_op jit(solution)/shard_map/all_to_all | solution.py:139
  74.7 127.4 %reduce-scatter.2.cloned.1.call-start = ((), (), s32[]{:S(2)}) async-start(), calls=%async_computation.5 | async-start | bytes 4456448 | tf_op jit(solution)/shard_map/reduce_scatter | solution.py:169
  75.3 12.5 %copy-start.6 = (f32[1,128,512]{2,0,1:T(1,128)}, f32[1,128,512]{2,0,1:T(1,128)S(1)}, u32[]{:S(2)}) copy-start(f32[1,128,512]{2,0,1:T(1,128)S(1)} %fusion.21) | copy-start | bytes 786436
  76.3 2.5 %copy-start.11 = (f32[1,255,512]{2,1,0:T(8,128)S(1)}, f32[1,255,512]{2,1,0:T(8,128)}, u32[]{:S(2)}) copy-start(f32[1,255,512]{2,1,0:T(8,128)} %fusion.9) | copy-start | bytes 1566724
  77.3 5.3 %copy-start.5 = (f32[2,16,4,512]{3,2,1,0:T(4,128)}, f32[2,16,4,512]{3,2,1,0:T(4,128)S(1)}, u32[]{:S(2)}) copy-start(f32[2,16,4,512]{3,2,1,0:T(4,128)S(1)} %copy.161) | copy-start | bytes 786436
  82.6 15.8 %copy-start.8 = (f32[1,128,512]{2,0,1:T(1,128)}, f32[1,128,512]{2,0,1:T(1,128)S(1)}, u32[]{:S(2)}) copy-start(f32[1,128,512]{2,0,1:T(1,128)S(1)} %fusion.14) | copy-start | bytes 786436
  85.9 11.3 %collective-permute-start.2 = (bf16[8,128,256]{1,2,0:T(8,128)(2,1)S(1)}, bf16[8,128,256]{1,2,0:T(8,128)(2,1)}, u32[]{:S(2)}, u32[]{:S(2)}) collective-permute-start(bf16[8,128,256]{1,2,0:T(8,128)(2,1)S(1)} %dynamic-slice_bitcast_fusion), channel_id=1, source_target_pairs={{0,32},{32,0},{1,33},{33,1},{2,34},{34,2},{3,35},{35,3},{4,36},{36... | collective-permute-start | bytes 1572872 | tf_op jit(solution)/shard_map/ppermute | solution.py:28
  87.9 9.3 %collective-permute-start.4 = (bf16[128,512]{1,0:T(8,128)(2,1)S(1)}, bf16[128,512]{1,0:T(8,128)(2,1)S(1)}, u32[]{:S(2)}, u32[]{:S(2)}) collective-permute-start(bf16[128,512]{1,0:T(8,128)(2,1)S(1)} %fusion.16), channel_id=1, source_target_pairs={{0,16},{16,0},{1,17},{17,1},{2,18},{18,2},{3,19},{19,3},{4,20},{20... | collective-permute-start | bytes 393224 | tf_op jit(solution)/shard_map/ppermute | solution.py:28
  100.5 2.0 copy-start
  103.0 1.6 copy-start.1
  105.8 7.4 %copy-start.2 = (bf16[8192,128]{1,0:T(8,128)(2,1)S(1)}, bf16[8192,128]{1,0:T(8,128)(2,1)}, u32[]{:S(2)}) copy-start(bf16[8192,128]{1,0:T(8,128)(2,1)} %all-gather.4.cloned.1.call-done) | copy-start | bytes 6291460
  105.9 15.4 %collective-permute-start.5 = (bf16[128,512]{1,0:T(8,128)(2,1)S(1)}, bf16[128,512]{1,0:T(8,128)(2,1)}, u32[]{:S(2)}, u32[]{:S(2)}) collective-permute-start(bf16[128,512]{1,0:T(8,128)(2,1)S(1)} %get-tuple-element.17), channel_id=1, source_target_pairs={{0,16},{16,0},{1,17},{17,1},{2,18},{18,2},{3,19},{19,3},{4,20},{20... | collective-permute-start | bytes 393224 | tf_op jit(solution)/shard_map/ppermute | solution.py:28
  115.5 5.7 %copy-start.7 = (f32[1,128,512]{2,0,1:T(1,128)S(1)}, f32[1,128,512]{2,0,1:T(1,128)}, u32[]{:S(2)}) copy-start(f32[1,128,512]{2,0,1:T(1,128)} %copy-done.6) | copy-start | bytes 786436
  115.5 5.7 %copy-start.9 = (f32[1,128,512]{2,0,1:T(1,128)S(1)}, f32[1,128,512]{2,0,1:T(1,128)}, u32[]{:S(2)}) copy-start(f32[1,128,512]{2,0,1:T(1,128)} %copy-done.8) | copy-start | bytes 786436
  115.5 8.2 %copy-start.12 = (f32[1,255,512]{2,1,0:T(8,128)S(1)}, f32[1,255,512]{2,1,0:T(8,128)}, u32[]{:S(2)}) copy-start(f32[1,255,512]{2,1,0:T(8,128)} %fusion.9) | copy-start | bytes 1566724
  115.5 41.6 %all-to-all-start.2 = ((bf16[16,128,256]{2,1,0:T(8,128)(2,1)}), bf16[16,128,256]{2,1,0:T(8,128)(2,1)S(1)}, u32[]{:S(2)}, u32[]{:S(2)}) async-start(bf16[16,128,256]{2,1,0:T(8,128)(2,1)} %shard_map.94), calls=%async_computation.2 | async-start | bytes 2097152 | tf_op jit(solution)/shard_map/all_to_all | solution.py:189
  122.3 9.5 %collective-permute-start.6 = (bf16[128,512]{1,0:T(8,128)(2,1)S(1)}, bf16[128,512]{1,0:T(8,128)(2,1)S(1)}, u32[]{:S(2)}, u32[]{:S(2)}) collective-permute-start(bf16[128,512]{1,0:T(8,128)(2,1)S(1)} %get-tuple-element.53), channel_id=1, source_target_pairs={{1,0},{2,1},{3,2},{4,3},{5,4},{6,5},{7,6},{8,7},{9,8},{10,9},{11,1... | collective-permute-start | bytes 393224 | tf_op jit(solution)/shard_map/ppermute | solution.py:24
  131.8 2.8 %copy-start.4 = (f32[1,256,1024]{2,1,0:T(8,128)S(1)}, f32[1,256,1024]{2,1,0:T(8,128)}, u32[]{:S(2)}) copy-start(f32[1,256,1024]{2,1,0:T(8,128)} %copy-done.3) | copy-start | bytes 3145732
  134.7 1.6 copy-start.10
  134.9 17.9 %collective-permute-start.9 = (f32[6,1536]{1,0:T(8,128)S(1)}, f32[6,1536]{1,0:T(8,128)S(1)}, u32[]{:S(2)}, u32[]{:S(2)}) collective-permute-start(f32[6,1536]{1,0:T(8,128)S(1)} %slice.113), channel_id=1, source_target_pairs={{1,0},{2,1},{3,2},{4,3},{5,4},{6,5},{7,6},{8,7},{9,8},{10,9},{11,1... | collective-permute-start | bytes 110600 | tf_op jit(solution)/shard_map/ppermute | solution.py:24
  138.8 17.5 %collective-permute-start.7 = (f32[88,512]{1,0:T(8,128)S(1)}, f32[88,512]{1,0:T(8,128)S(1)}, u32[]{:S(2)}, u32[]{:S(2)}) collective-permute-start(f32[88,512]{1,0:T(8,128)S(1)} %pad_maximum_fusion.4), channel_id=1, source_target_pairs={{0,16},{16,0},{1,17},{17,1},{2,18},{18,2},{3,19},{19,3},{4,20},{20... | collective-permute-start | bytes 540680 | tf_op jit(solution)/shard_map/ppermute | solution.py:28
  154.0 6.8 %copy-start.16 = (f32[3,7,512]{2,1,0:T(8,128)S(1)}, f32[3,7,512]{2,1,0:T(8,128)}, u32[]{:S(2)}) copy-start(f32[3,7,512]{2,1,0:T(8,128)} %param.6) | copy-start | bytes 129028
  154.0 6.8 %copy-start.18 = (pred[8,17]{0,1:T(8,128)(4,1)S(1)}, pred[8,17]{0,1:T(8,128)(4,1)}, u32[]{:S(2)}) copy-start(pred[8,17]{0,1:T(8,128)(4,1)} %constant.53) | copy-start | bytes 412
  157.1 44.3 %all-to-all-start.3 = ((f32[16,4,512]{2,1,0:T(4,128)}), f32[16,4,512]{2,1,0:T(4,128)S(1)}, u32[]{:S(2)}, u32[]{:S(2)}) async-start(f32[16,4,512]{2,1,0:T(4,128)} %bitcast_add_fusion), calls=%async_computation.3 | async-start | bytes 262144 | tf_op jit(solution)/shard_map/all_to_all | solution.py:211
  162.8 38.6 %collective-permute-start.8 = (bf16[128,256]{1,0:T(8,128)(2,1)S(1)}, bf16[128,256]{1,0:T(8,128)(2,1)S(1)}, u32[]{:S(2)}, u32[]{:S(2)}) collective-permute-start(bf16[128,256]{1,0:T(8,128)(2,1)S(1)} %reduce_sum.30), channel_id=1, source_target_pairs={{0,0},{1,1},{2,2},{3,3},{4,4},{5,5},{6,6},{7,7},{8,8},{9,9},{10,10... | collective-permute-start | bytes 196616 | tf_op jit(solution)/shard_map/ppermute | solution.py:214
Sparse Core Ops, SparseCore 0:
  23.5 79.5 all-gather.3
  106.4 82.1 reduce-scatter.1

commit v3 on v2

--- a/solution.py
+++ b/solution.py
@@ -127,10 +127,15 @@
     yh = lax.axis_index("yh")
     co = lax.axis_index("co")
 
+    inputs = qkv.reshape(rows, 3 * channels)
+    reach = reach_short - 1
+    input_rim = passed_along(inputs[rows - reach :], 1)
+
     gathered = lax.all_gather(proj, ALONG, axis=0, tiled=False)
 
     taps_pair = ordered(yh, long_filter, swapped(long_filter, "yh"))
     taps_copies = jnp.broadcast_to(taps_pair[None], (ZS,) + taps_pair.shape)
+    taps_copies = after(taps_copies, input_rim)
     taps_all = lax.all_to_all(taps_copies, ALONG, 0, 0, tiled=True)
     long_taps = jnp.transpose(taps_all, (1, 0, 2, 3)).reshape(2 * ZS * taps_here, channels)
     reach_long = long_taps.shape[0]
@@ -142,22 +147,15 @@
     both = ordered(co, half, swapped(half, "co")).reshape(2, 2, 2, 2, rows, 2, WIDE)
     grads = jnp.transpose(both, (1, 2, 0, 5, 3, 4, 6)).reshape(ZS, 2 * rows, WIDE)
 
-    inputs = qkv.reshape(rows, 3 * channels)
-    reach = reach_short - 1
-    sent = jnp.concatenate([inputs[:, channels:], inputs[rows - 8 :, :channels].reshape(4, 2 * channels)], axis=0)
-    before = passed_along(sent, 1)
-    far = passed_along(inputs[rows - 8 :, channels:], 2)
-    query_rim = before[rows:].reshape(8, channels)[8 - reach :]
-    before = before[:rows]
-    rim = jnp.concatenate([query_rim, before[rows - reach :]], axis=1)
-    extended = jnp.concatenate([rim, inputs], axis=0).astype(F32)
+    extended = jnp.concatenate([input_rim, inputs], axis=0).astype(F32)
     short_taps = jnp.transpose(short_filter, (1, 0, 2)).reshape(reach_short, 3 * channels)
-    query_side = depthwise(extended[:, :channels], short_taps[::-1, :channels])
-    pairs = jnp.concatenate([far[8 - reach :], before, inputs[:, channels:]], axis=0)
-    pairs = depthwise(pairs.astype(F32), short_taps[::-1, channels:])
-    key_side = pairs[rows:, :channels]
-    value_side = pairs[rows:, channels:]
-    product_ext = (pairs[:, :channels] * pairs[:, channels:])[2 * rows - (rows + reach_long - 1) :]
+    short_out = depthwise(extended, short_taps[::-1])
+    query_side = short_out[:, :channels]
+    key_side = short_out[:, channels : 2 * channels]
+    value_side = short_out[:, 2 * channels :]
+    product = key_side * value_side
+    product_rim = passed_along(product[rows - reach_long + 1 :], 1)
+    product_ext = jnp.concatenate([product_rim, product], axis=0)
 
     long_mix = depthwise(product_ext, long_taps[::-1])
     gated_out = (query_side * long_mix).astype(BF16)
@@ -195,26 +193,27 @@
     mixed_ext = jnp.concatenate([mixed_grad, after(mixed_rim, out_part, long_part)], axis=0)
     product_grad = depthwise(mixed_ext, long_taps)
     short_grad = jnp.concatenate([query_grad, product_grad * value_side, product_grad * key_side], axis=1)
-    short_rim = passed_along(short_grad[: reach_short - 1], -1)
+    short_part = depthwise(extended, short_grad)[::-1]
+    short_rim = passed_along(after(short_grad[: reach_short - 1], short_part), -1)
     grad_inputs = depthwise(jnp.concatenate([short_grad, short_rim], axis=0), short_taps)
     grad_qkv = grad_inputs.reshape(rows, 3, channels).astype(BF16)
-    short_part = depthwise(extended, short_grad)[::-1]
-
-    short_rows = jnp.pad(short_part.reshape(3 * reach_short, channels), ((0, 3), (0, 0)))
+
+    short_rows = jnp.pad(short_part.reshape(3 * reach_short, channels), ((0, 32 - 3 * reach_short), (0, 0)))
+    short_rows = short_rows.reshape(ZS, 2, channels)
     long_kept = lax.dynamic_index_in_dim(long_part, yh, 0, keepdims=False)
     long_given = lax.dynamic_index_in_dim(long_part, 1 - yh, 0, keepdims=False)
-    terms_given = jnp.concatenate([long_given.reshape(ZS * taps_here, channels), short_rows], axis=0)
-    terms_got = swapped(terms_given, "yh")
-    long_half = long_kept + terms_got[: ZS * taps_here].reshape(long_kept.shape)
-    short_pair = (short_rows + terms_got[ZS * taps_here :]).astype(BF16)
-    short_pair, out_terms, long_half = lax.optimization_barrier((short_pair, out_terms, long_half))
-    grad_long = jnp.sum(lax.all_to_all(long_half, ALONG, 0, 0, tiled=True), axis=0)
+    terms_got = swapped(jnp.concatenate([long_given, short_rows], axis=1).astype(BF16), "yh")
+    terms = jnp.concatenate([long_kept, short_rows], axis=1) + terms_got.astype(F32)
+    terms = terms.astype(BF16)
+    terms, out_terms = lax.optimization_barrier((terms, out_terms))
+    sums = jnp.sum(lax.all_to_all(terms, ALONG, 0, 0, tiled=True).astype(F32), axis=0)
+    grad_long = sums[:taps_here]
+    short_copies = jnp.broadcast_to(sums[None, taps_here:], (ZS, 2, channels))
+    short_sum = lax.all_to_all(short_copies, ALONG, 0, 0, tiled=True).reshape(2 * ZS, channels)
+    grad_short = jnp.transpose(short_sum[: 3 * reach_short].reshape(reach_short, 3, channels), (1, 0, 2))
 
     out_sum = jnp.sum(out_terms.astype(F32), axis=0).astype(BF16)
     layer_out = lax.ppermute(out_sum, AXES, owner_pairs())
-
-    short_sum = jnp.sum(lax.all_gather(short_pair, ALONG, axis=0, tiled=False).astype(F32), axis=0)
-    grad_short = jnp.transpose(short_sum[: 3 * reach_short].reshape(reach_short, 3, channels), (1, 0, 2))
     return (layer_out, grad_qkv, grad_short, grad_long, grad_proj)
 
 

time: 211 us -> 198 us (0.938)
  blocking collectives: 32.2 us -> 0 us
  waiting for transfers between devices: 41.9 us -> 63.1 us
  starting transfers between devices: 72.9 us -> 76 us
  local copies, waits for them, and re-layouts: 22 us -> 19.7 us
    all_gather x1 -> x0, blocking collectives: 32.2 us -> none  [local(): lax.all_gather(short_pair, ALONG, axis=0, tiled=False).astype(F32)]
    all_to_all x1 -> x2, waiting for transfers between devices: 0.01 us -> 14.9 us  [the longest x1 14.1 us: local(): lax.all_to_all(terms, ALONG, 0, 0, tiled=True).astype(F32)]
    all_to_all x1, waiting for transfers between devices: 25 us -> 14.1 us  [local(): taps_all = lax.all_to_all(taps_copies, ALONG, 0, 0, tiled=True)]
    all_to_all x1 -> x2, starting transfers between devices: 3.6 us -> 13.7 us  [the longest x1 9.46 us: local(): lax.all_to_all(terms, ALONG, 0, 0, tiled=True).astype(F32)]
    ppermute x5, starting transfers between devices: 28.3 us -> 19.6 us  [swapped(): return lax.ppermute(value, axis, [(0, 1), (1, 0)])]
    ppermute x4, waiting for transfers between devices: 4.79 us -> 13.5 us  [passed_along(): lax.ppermute(value, CTX, [(source, source + steps) for source in range(fi...]
    all_to_all x1, waiting for transfers between devices: 3.28 us -> 7.91 us  [local(): blocks = lax.all_to_all(copies, ('x', 'yl', 'yh'), 0, 0, tiled=True)]
    all_to_all x1, starting transfers between devices: 12.5 us -> 17 us  [local(): taps_all = lax.all_to_all(taps_copies, ALONG, 0, 0, tiled=True)]
  transfers between devices with their start and end apart: 16 -> 17, of which waited for: 6 -> 9; matrix products, arithmetic and copies ran while one was open for 18% -> 16% of each run, Pallas kernels for 2% -> 2%
where the time goes in v3:
time: 198 us; the launch traced here: 196 us
  starting transfers between devices  76 us (38%)
  waiting for transfers between devices  63.1 us (32%)
  local copies, waits for them, and re-layouts  19.7 us (10%)
  between operations  14.9 us (8%)
  matrix products  12.8 us (6%)
  other arithmetic  5.31 us (3%)
  Pallas kernels  4.78 us (2%)
    ppermute x5, starting transfers between devices, swapped(): return lax.ppermute(value, axis, [(0, 1), (1, 0)])  19.6 us
    all_to_all x1, starting transfers between devices, local(): taps_all = lax.all_to_all(taps_copies, ALONG, 0, 0, tiled=True)  17 us
    all_to_all x1, waiting for transfers between devices, local(): lax.all_to_all(terms, ALONG, 0, 0, tiled=True).astype(F32)  14.1 us
    all_to_all x1, waiting for transfers between devices, local(): taps_all = lax.all_to_all(taps_copies, ALONG, 0, 0, tiled=True)  14.1 us
    ppermute x4, waiting for transfers between devices, passed_along(): lax.ppermute(value, CTX, [(source, source + steps) for source in range(fi...  13.5 us
    conv_general_dilated x6, matrix products, depthwise(): lax.conv_general_dilated(padded[None], kernel[:, None, :], (1,), 'VALID',...  12.8 us
    ppermute x4, starting transfers between devices, passed_along(): lax.ppermute(value, CTX, [(source, source + steps) for source in range(fi...  10.3 us
    all_to_all x1, starting transfers between devices, local(): lax.all_to_all(terms, ALONG, 0, 0, tiled=True).astype(F32)  9.46 us
  transfers between devices with their start and end apart: 17, of which 9 were waited for; matrix products, arithmetic and copies ran while one was open for 16% of the time, Pallas kernels for 2%

profile of v3, /device:TPU:6, one launch (start us, length us, event | category | flops | bytes accessed | tf_op | source)
XLA Modules:
  0.0 196.5 jit_solution(1611318238522673612)
XLA Ops:
  7.9 5.1 %collective-permute-start.2 = (f32[4,512]{1,0:T(4,128)}, f32[4,512]{1,0:T(4,128)S(1)}, u32[]{:S(2)}, u32[]{:S(2)}) collective-permute-start(f32[4,512]{1,0:T(4,128)} %param.7), channel_id=1, source_target_pairs={{0,16},{16,0},{1,17},{17,1},{2,18},{18,2},{3,19},{19,3},{4,20},{20... | collective-permute-start | bytes 24584 | tf_op jit(solution)/shard_map/ppermute | solution.py:28
  13.0 0.7 slice.36
  14.0 3.8 %collective-permute-start = (bf16[6,1536]{0,1:T(8,128)(2,1)S(1)}, bf16[6,1536]{0,1:T(8,128)(2,1)S(1)}, u32[]{:S(2)}, u32[]{:S(2)}) collective-permute-start(bf16[6,1536]{0,1:T(8,128)(2,1)S(1)} %bitcast.92), channel_id=1, source_target_pairs={{0,1},{1,2},{2,3},{3,4},{4,5},{5,6},{6,7},{7,8},{8,9},{9,10},{10,1... | collective-permute-start | bytes 55304 | tf_op jit(solution)/shard_map/ppermute | solution.py:24
  17.9 0.7 select_bitcast_fusion.3
  18.6 7.3 %collective-permute-done = bf16[6,1536]{0,1:T(8,128)(2,1)S(1)} collective-permute-done((bf16[6,1536]{0,1:T(8,128)(2,1)S(1)}, bf16[6,1536]{0,1:T(8,128)(2,1)S(1)}, u32[]{:S(2)}, u32[]{:S(2)}) %collective-permute-start) | collective-permute-done | bytes 18464 | tf_op jit(solution)/shard_map/ppermute | solution.py:24
  26.0 0.8 broadcast_in_dim.48
  26.7 17.0 %all-to-all-start = ((f32[16,2,4,512]{3,2,1,0:T(4,128)}), f32[16,2,4,512]{3,2,1,0:T(4,128)S(1)}, u32[]{:S(2)}, u32[]{:S(2)}) async-start(f32[16,2,4,512]{3,2,1,0:T(4,128)} %broadcast_in_dim.48), calls=%async_computation | async-start | bytes 524288 | tf_op jit(solution)/shard_map/all_to_all | solution.py:139
  44.6 0.9 copy.60
  45.6 0.9 copy-done.10
  46.4 1.6 fusion.26
  48.2 3.8 %collective-permute-start.1 = (f32[127,512]{1,0:T(8,128)S(1)}, f32[127,512]{1,0:T(8,128)S(1)}, u32[]{:S(2)}, u32[]{:S(2)}) collective-permute-start(f32[127,512]{1,0:T(8,128)S(1)} %slice.52), channel_id=1, source_target_pairs={{0,1},{1,2},{2,3},{3,4},{4,5},{5,6},{6,7},{7,8},{8,9},{9,10},{10,1... | collective-permute-start | bytes 780296 | tf_op jit(solution)/shard_map/ppermute | solution.py:24
  52.2 14.1 %all-to-all-done = f32[16,2,4,512]{3,2,1,0:T(4,128)S(1)} async-done(((f32[16,2,4,512]{3,2,1,0:T(4,128)}), f32[16,2,4,512]{3,2,1,0:T(4,128)S(1)}, u32[]{:S(2)}, u32[]{:S(2)}) %all-to-all-start) | async-done | bytes 262176 | tf_op jit(solution)/shard_map/all_to_all | solution.py:139
  66.3 1.2 broadcast_in_dim.47
  67.5 4.8 %all-to-all-start.1 = ((bf16[16,128,256]{1,2,0:T(8,128)(2,1)}), bf16[16,128,256]{1,2,0:T(8,128)(2,1)S(1)}, u32[]{:S(2)}, u32[]{:S(2)}) async-start(bf16[16,128,256]{1,2,0:T(8,128)(2,1)} %broadcast_in_dim.47), calls=%async_computation.1 | async-start | bytes 2097152 | tf_op jit(solution)/shard_map/all_to_all | solution.py:144
  72.7 2.9 %fusion.11 = f32[1,128,512]{2,0,1:T(1,128)S(1)} fusion(f32[1,255,512]{2,1,0:T(8,128)S(1)} %maximum_bitcast_fusion.3, f32[128,1,512]{2,0,1:T(8,128)S(1)} %bitcast.93), kind=kOutput, calls=%fused_computation.23 | convolution fusion | flops 100663296 | bytes 1046528 | tf_op jit(solution)/shard_map/conv_general_dilated | solution.py:42
  75.7 7.9 %all-to-all-done.1 = bf16[16,128,256]{1,2,0:T(8,128)(2,1)S(1)} async-done(((bf16[16,128,256]{1,2,0:T(8,128)(2,1)}), bf16[16,128,256]{1,2,0:T(8,128)(2,1)S(1)}, u32[]{:S(2)}, u32[]{:S(2)}) %all-to-all-start.1) | async-done | bytes 1048608 | tf_op jit(solution)/shard_map/all_to_all | solution.py:144
  83.6 1.9 collective-permute-start.3
  85.6 3.7 %collective-permute-start.4 = (bf16[128,512]{1,0:T(8,128)(2,1)S(1)}, bf16[128,512]{1,0:T(8,128)(2,1)S(1)}, u32[]{:S(2)}, u32[]{:S(2)}) collective-permute-start(bf16[128,512]{1,0:T(8,128)(2,1)S(1)} %fusion.16), channel_id=1, source_target_pairs={{0,16},{16,0},{1,17},{17,1},{2,18},{18,2},{3,19},{19,3},{4,20},{20... | collective-permute-start | bytes 393224 | tf_op jit(solution)/shard_map/ppermute | solution.py:28
  89.3 5.6 %collective-permute-done.4 = bf16[128,512]{1,0:T(8,128)(2,1)S(1)} collective-permute-done((bf16[128,512]{1,0:T(8,128)(2,1)S(1)}, bf16[128,512]{1,0:T(8,128)(2,1)S(1)}, u32[]{:S(2)}, u32[]{:S(2)}) %collective-permute-start.4) | collective-permute-done | bytes 131104 | tf_op jit(solution)/shard_map/ppermute | solution.py:28
  95.8 1.3 shard_map.92
  97.2 2.0 copy-done
  99.2 1.6 copy-done.1
  100.8 1.2 shard_map.93
  102.0 0.7 copy-done.3
  102.7 3.7 %collective-permute-start.5 = (bf16[128,512]{1,0:T(8,128)(2,1)S(1)}, bf16[128,512]{1,0:T(8,128)(2,1)}, u32[]{:S(2)}, u32[]{:S(2)}) collective-permute-start(bf16[128,512]{1,0:T(8,128)(2,1)S(1)} %get-tuple-element.19), channel_id=1, source_target_pairs={{0,16},{16,0},{1,17},{17,1},{2,18},{18,2},{3,19},{19,3},{4,20},{20... | collective-permute-start | bytes 393224 | tf_op jit(solution)/shard_map/ppermute | solution.py:28
  106.4 2.0 %broadcast_in_dim_reshape.6 = f32[128,1,512]{2,1,0:T(1,128)} reshape(f32[2,16,4,512]{3,2,1,0:T(4,128)} %copy-done.7) | data formatting | bytes 524288 | tf_op jit(solution)/shard_map/broadcast_in_dim;reshape | solution.py:44
  108.5 2.2 %shard_map.94 = bf16[16,128,256]{2,1,0:T(8,128)(2,1)} custom-call(bf16[256,512]{1,0:T(8,128)(2,1)S(1)} %bitcast.78, bf16[16,512,128]{2,1,0:T(8,128)(2,1)S(1)} %bitcast.76), custom_call_target="tpu_custom_call" | custom-call | flops 536870912 | bytes 3407872 | tf_op jit(solution)/shard_map/pallas_call | solution.py:105
  110.7 5.7 %all-to-all-start.2 = ((bf16[16,128,256]{2,1,0:T(8,128)(2,1)}), bf16[16,128,256]{2,1,0:T(8,128)(2,1)S(1)}, u32[]{:S(2)}, u32[]{:S(2)}) async-start(bf16[16,128,256]{2,1,0:T(8,128)(2,1)} %shard_map.94), calls=%async_computation.2 | async-start | bytes 2097152 | tf_op jit(solution)/shard_map/all_to_all | solution.py:187
  116.4 1.7 fusion.25
  118.2 1.3 collective-permute-start.6
  119.5 2.9 %fusion.13 = f32[1,128,512]{2,0,1:T(1,128)S(1)} fusion(f32[1,255,512]{2,1,0:T(8,128)S(1)} %copy-done.13, f32[128,1,512]{2,0,1:T(8,128)S(1)} %bitcast.91), kind=kOutput, calls=%fused_computation.25 | convolution fusion | flops 100663296 | bytes 1046528 | tf_op jit(solution)/shard_map/conv_general_dilated | solution.py:42
  122.7 6.2 %collective-permute-done.6 = bf16[128,512]{1,0:T(8,128)(2,1)} collective-permute-done((bf16[128,512]{1,0:T(8,128)(2,1)}, bf16[128,512]{1,0:T(8,128)(2,1)}, u32[]{:S(2)}, u32[]{:S(2)}) %collective-permute-start.6) | collective-permute-done | bytes 131104 | tf_op jit(solution)/shard_map/ppermute | solution.py:24
  128.9 0.9 slice_convert_fusion
  129.9 2.8 %fusion.9 = f32[1,128,512]{2,0,1:T(1,128)S(1)} fusion(f32[128,1,512]{2,1,0:T(1,128)S(1)} %copy-done.15, f32[1,255,512]{2,1,0:T(8,128)S(1)} %maximum_bitcast_fusion.4), kind=kOutput, calls=%fused_computation.21 | convolution fusion | flops 100663296 | bytes 1046528 | tf_op jit(solution)/shard_map/conv_general_dilated | solution.py:42
  132.9 1.0 copy-done.11
  133.9 2.1 %fusion.5 = f32[1,7,1536]{2,0,1:T(1,128)S(1)} fusion(bf16[1,134,1536]{2,0,1:T(2,128)(2,1)S(1)} %copy-done.11, f32[128,1,1536]{2,0,1:T(8,128)S(1)} %get-tuple-element.47), kind=kOutput, calls=%fused_computation.12 | convolution fusion | flops 16515072 | bytes 1241088 | tf_op jit(solution)/shard_map/conv_general_dilated | solution.py:42
  136.5 5.1 %collective-permute-start.7 = (bf16[16,6,512]{2,1,0:T(8,128)(2,1)S(1)}, bf16[16,6,512]{2,1,0:T(8,128)(2,1)S(1)}, u32[]{:S(2)}, u32[]{:S(2)}) collective-permute-start(bf16[16,6,512]{2,1,0:T(8,128)(2,1)S(1)} %pad_maximum_fusion.2), channel_id=1, source_target_pairs={{0,16},{16,0},{1,17},{17,1},{2,18},{18,2},{3,19},{19,3},{4,20},{20... | collective-permute-start | bytes 294920 | tf_op jit(solution)/shard_map/ppermute | solution.py:28
  141.7 3.2 %collective-permute-done.7 = bf16[16,6,512]{2,1,0:T(8,128)(2,1)S(1)} collective-permute-done((bf16[16,6,512]{2,1,0:T(8,128)(2,1)S(1)}, bf16[16,6,512]{2,1,0:T(8,128)(2,1)S(1)}, u32[]{:S(2)}, u32[]{:S(2)}) %collective-permute-start.7) | collective-permute-done | bytes 98336 | tf_op jit(solution)/shard_map/ppermute | solution.py:28
  144.9 0.7 fusion.15
  145.6 9.5 %all-to-all-start.3 = ((bf16[16,6,512]{2,1,0:T(8,128)(2,1)}), bf16[16,6,512]{2,1,0:T(8,128)(2,1)S(1)}, u32[]{:S(2)}, u32[]{:S(2)}) async-start(bf16[16,6,512]{2,1,0:T(8,128)(2,1)} %fusion.15), calls=%async_computation.3 | async-start | bytes 262144 | tf_op jit(solution)/shard_map/all_to_all | solution.py:209
  155.1 1.3 collective-permute-start.9
  156.4 14.1 %all-to-all-done.3 = bf16[16,6,512]{2,1,0:T(8,128)(2,1)S(1)} async-done(((bf16[16,6,512]{2,1,0:T(8,128)(2,1)}), bf16[16,6,512]{2,1,0:T(8,128)(2,1)S(1)}, u32[]{:S(2)}, u32[]{:S(2)}) %all-to-all-start.3) | async-done | bytes 98336 | tf_op jit(solution)/shard_map/all_to_all | solution.py:209
  171.2 4.2 %all-to-all-start.4 = ((f32[16,2,512]{2,1,0:T(2,128)}), f32[16,2,512]{2,1,0:T(2,128)S(1)}, u32[]{:S(2)}, u32[]{:S(2)}) async-start(f32[16,2,512]{2,1,0:T(2,128)} %broadcast_in_dim.54), calls=%async_computation.4 | async-start | bytes 131072 | tf_op jit(solution)/shard_map/all_to_all | solution.py:212
  175.6 1.0 reshape.74
  176.9 5.0 %collective-permute-start.8 = (bf16[128,256]{1,0:T(8,128)(2,1)S(1)}, bf16[128,256]{1,0:T(8,128)(2,1)S(1)}, u32[]{:S(2)}, u32[]{:S(2)}) collective-permute-start(bf16[128,256]{1,0:T(8,128)(2,1)S(1)} %reduce_sum.21), channel_id=1, source_target_pairs={{0,0},{1,1},{2,2},{3,3},{4,4},{5,5},{6,6},{7,7},{8,8},{9,9},{10,10... | collective-permute-start | bytes 196616 | tf_op jit(solution)/shard_map/ppermute | solution.py:216
  182.9 0.9 copy.77
  183.8 3.1 %collective-permute-done.8 = bf16[128,256]{1,0:T(8,128)(2,1)S(1)} collective-permute-done((bf16[128,256]{1,0:T(8,128)(2,1)S(1)}, bf16[128,256]{1,0:T(8,128)(2,1)S(1)}, u32[]{:S(2)}, u32[]{:S(2)}) %collective-permute-start.8) | collective-permute-done | bytes 65568 | tf_op jit(solution)/shard_map/ppermute | solution.py:216
  187.6 0.7 all-to-all-done.4
  (103 shorter events, 8.5 us)
Async XLA Ops:
  7.2 36.5 %copy-start.14 = (bf16[128,3,512]{2,0,1:T(8,128)(2,1)S(1)}, bf16[128,3,512]{2,0,1:T(8,128)(2,1)}, u32[]{:S(2)}) copy-start(bf16[128,3,512]{2,0,1:T(8,128)(2,1)} %param.5) | copy-start | bytes 1179652
  7.2 36.7 %copy-start.17 = (f32[3,7,512]{2,1,0:T(8,128)S(1)}, f32[3,7,512]{2,1,0:T(8,128)}, u32[]{:S(2)}) copy-start(f32[3,7,512]{2,1,0:T(8,128)} %param.6) | copy-start | bytes 129028
  7.2 92.0 %all-gather.3.cloned.1.call-start = ((), (), s32[]{:S(2)}) async-start(), calls=%async_computation.7 | async-start | bytes 2228224 | tf_op jit(solution)/shard_map/all_gather | solution.py:134
  7.9 10.0 %collective-permute-start.2 = (f32[4,512]{1,0:T(4,128)}, f32[4,512]{1,0:T(4,128)S(1)}, u32[]{:S(2)}, u32[]{:S(2)}) collective-permute-start(f32[4,512]{1,0:T(4,128)} %param.7), channel_id=1, source_target_pairs={{0,16},{16,0},{1,17},{17,1},{2,18},{18,2},{3,19},{19,3},{4,20},{20... | collective-permute-start | bytes 24584 | tf_op jit(solution)/shard_map/ppermute | solution.py:28
  14.0 11.9 %collective-permute-start = (bf16[6,1536]{0,1:T(8,128)(2,1)S(1)}, bf16[6,1536]{0,1:T(8,128)(2,1)S(1)}, u32[]{:S(2)}, u32[]{:S(2)}) collective-permute-start(bf16[6,1536]{0,1:T(8,128)(2,1)S(1)} %bitcast.92), channel_id=1, source_target_pairs={{0,1},{1,2},{2,3},{3,4},{4,5},{5,6},{6,7},{7,8},{8,9},{9,10},{10,1... | collective-permute-start | bytes 55304 | tf_op jit(solution)/shard_map/ppermute | solution.py:24
  26.7 39.6 %all-to-all-start = ((f32[16,2,4,512]{3,2,1,0:T(4,128)}), f32[16,2,4,512]{3,2,1,0:T(4,128)S(1)}, u32[]{:S(2)}, u32[]{:S(2)}) async-start(f32[16,2,4,512]{3,2,1,0:T(4,128)} %broadcast_in_dim.48), calls=%async_computation | async-start | bytes 524288 | tf_op jit(solution)/shard_map/all_to_all | solution.py:139
  45.5 0.9 copy-start.10
  48.1 4.0 %copy-start.16 = (bf16[128,256]{1,0:T(8,128)(2,1)S(1)}, bf16[128,256]{1,0:T(8,128)(2,1)}, u32[]{:S(2)}) copy-start(bf16[128,256]{1,0:T(8,128)(2,1)} %param.9) | copy-start | bytes 196612
  48.1 37.4 %copy-start.5 = (f32[1,128,1536]{2,1,0:T(8,128)}, f32[1,128,1536]{2,1,0:T(8,128)S(1)}, u32[]{:S(2)}) copy-start(f32[1,128,1536]{2,1,0:T(8,128)S(1)} %copy.107) | copy-start | bytes 2359300
  48.2 24.2 %collective-permute-start.1 = (f32[127,512]{1,0:T(8,128)S(1)}, f32[127,512]{1,0:T(8,128)S(1)}, u32[]{:S(2)}, u32[]{:S(2)}) collective-permute-start(f32[127,512]{1,0:T(8,128)S(1)} %slice.52), channel_id=1, source_target_pairs={{0,1},{1,2},{2,3},{3,4},{4,5},{5,6},{6,7},{7,8},{8,9},{9,10},{10,1... | collective-permute-start | bytes 780296 | tf_op jit(solution)/shard_map/ppermute | solution.py:24
  67.5 16.1 %all-to-all-start.1 = ((bf16[16,128,256]{1,2,0:T(8,128)(2,1)}), bf16[16,128,256]{1,2,0:T(8,128)(2,1)S(1)}, u32[]{:S(2)}, u32[]{:S(2)}) async-start(bf16[16,128,256]{1,2,0:T(8,128)(2,1)} %broadcast_in_dim.47), calls=%async_computation.1 | async-start | bytes 2097152 | tf_op jit(solution)/shard_map/all_to_all | solution.py:144
  72.3 116.7 %reduce-scatter.2.cloned.1.call-start = ((), (), s32[]{:S(2)}) async-start(), calls=%async_computation.6 | async-start | bytes 4456448 | tf_op jit(solution)/shard_map/reduce_scatter | solution.py:167
  72.4 3.2 %copy-start.12 = (f32[1,255,512]{2,1,0:T(8,128)}, f32[1,255,512]{2,1,0:T(8,128)S(1)}, u32[]{:S(2)}) copy-start(f32[1,255,512]{2,1,0:T(8,128)S(1)} %maximum_bitcast_fusion.3) | copy-start | bytes 1566724
  72.5 3.2 %copy-start.7 = (f32[2,16,4,512]{3,2,1,0:T(4,128)}, f32[2,16,4,512]{3,2,1,0:T(4,128)S(1)}, u32[]{:S(2)}) copy-start(f32[2,16,4,512]{3,2,1,0:T(4,128)S(1)} %copy.63) | copy-start | bytes 786436
  75.7 19.3 %copy-start.8 = (f32[1,128,512]{2,0,1:T(1,128)}, f32[1,128,512]{2,0,1:T(1,128)S(1)}, u32[]{:S(2)}) copy-start(f32[1,128,512]{2,0,1:T(1,128)S(1)} %fusion.11) | copy-start | bytes 786436
  83.6 11.4 %collective-permute-start.3 = (bf16[8,128,256]{1,2,0:T(8,128)(2,1)S(1)}, bf16[8,128,256]{1,2,0:T(8,128)(2,1)S(1)}, u32[]{:S(2)}, u32[]{:S(2)}) collective-permute-start(bf16[8,128,256]{1,2,0:T(8,128)(2,1)S(1)} %dynamic-slice_bitcast_fusion), channel_id=1, source_target_pairs={{0,32},{32,0},{1,33},{33,1},{2,34},{34,2},{3,35},{35,3},{4,36},{36... | collective-permute-start | bytes 1572872 | tf_op jit(solution)/shard_map/ppermute | solution.py:28
  85.6 9.3 %collective-permute-start.4 = (bf16[128,512]{1,0:T(8,128)(2,1)S(1)}, bf16[128,512]{1,0:T(8,128)(2,1)S(1)}, u32[]{:S(2)}, u32[]{:S(2)}) collective-permute-start(bf16[128,512]{1,0:T(8,128)(2,1)S(1)} %fusion.16), channel_id=1, source_target_pairs={{0,16},{16,0},{1,17},{17,1},{2,18},{18,2},{3,19},{19,3},{4,20},{20... | collective-permute-start | bytes 393224 | tf_op jit(solution)/shard_map/ppermute | solution.py:28
  97.2 2.0 %copy-start = (f32[16,512,128]{2,1,0:T(8,128)}, f32[16,512,128]{2,1,0:T(8,128)S(1)}, u32[]{:S(2)}) copy-start(f32[16,512,128]{2,1,0:T(8,128)S(1)} %shard_map.92) | copy-start | bytes 12582916
  99.2 1.6 copy-start.1
  100.8 7.7 %copy-start.2 = (bf16[8192,128]{1,0:T(8,128)(2,1)S(1)}, bf16[8192,128]{1,0:T(8,128)(2,1)}, u32[]{:S(2)}) copy-start(bf16[8192,128]{1,0:T(8,128)(2,1)} %all-gather.3.cloned.1.call-done) | copy-start | bytes 6291460
  102.0 0.7 copy-start.3
  102.7 13.7 %collective-permute-start.5 = (bf16[128,512]{1,0:T(8,128)(2,1)S(1)}, bf16[128,512]{1,0:T(8,128)(2,1)}, u32[]{:S(2)}, u32[]{:S(2)}) collective-permute-start(bf16[128,512]{1,0:T(8,128)(2,1)S(1)} %get-tuple-element.19), channel_id=1, source_target_pairs={{0,16},{16,0},{1,17},{17,1},{2,18},{18,2},{3,19},{19,3},{4,20},{20... | collective-permute-start | bytes 393224 | tf_op jit(solution)/shard_map/ppermute | solution.py:28
  110.7 5.7 %copy-start.4 = (f32[128,512]{1,0:T(8,128)S(1)}, f32[128,512]{1,0:T(8,128)}, u32[]{:S(2)}) copy-start(f32[128,512]{1,0:T(8,128)} %copy-done.3) | copy-start | bytes 786436
  110.7 5.7 %copy-start.6 = (f32[1,128,1536]{2,1,0:T(8,128)S(1)}, f32[1,128,1536]{2,1,0:T(8,128)}, u32[]{:S(2)}) copy-start(f32[1,128,1536]{2,1,0:T(8,128)} %copy-done.5) | copy-start | bytes 2359300
  110.7 5.7 %copy-start.9 = (f32[1,128,512]{2,0,1:T(1,128)S(1)}, f32[1,128,512]{2,0,1:T(1,128)}, u32[]{:S(2)}) copy-start(f32[1,128,512]{2,0,1:T(1,128)} %copy-done.8) | copy-start | bytes 786436
  110.7 34.9 %all-to-all-start.2 = ((bf16[16,128,256]{2,1,0:T(8,128)(2,1)}), bf16[16,128,256]{2,1,0:T(8,128)(2,1)S(1)}, u32[]{:S(2)}, u32[]{:S(2)}) async-start(bf16[16,128,256]{2,1,0:T(8,128)(2,1)} %shard_map.94), calls=%async_computation.2 | async-start | bytes 2097152 | tf_op jit(solution)/shard_map/all_to_all | solution.py:187
  116.4 3.0 %copy-start.13 = (f32[1,255,512]{2,1,0:T(8,128)S(1)}, f32[1,255,512]{2,1,0:T(8,128)}, u32[]{:S(2)}) copy-start(f32[1,255,512]{2,1,0:T(8,128)} %copy-done.12) | copy-start | bytes 1566724
  118.2 10.7 %collective-permute-start.6 = (bf16[128,512]{1,0:T(8,128)(2,1)}, bf16[128,512]{1,0:T(8,128)(2,1)}, u32[]{:S(2)}, u32[]{:S(2)}) collective-permute-start(bf16[128,512]{1,0:T(8,128)(2,1)} %get-tuple-element.40), channel_id=1, source_target_pairs={{1,0},{2,1},{3,2},{4,3},{5,4},{6,5},{7,6},{8,7},{9,8},{10,9},{11,1... | collective-permute-start | bytes 393224 | tf_op jit(solution)/shard_map/ppermute | solution.py:24
  122.5 7.3 %copy-start.15 = (f32[128,1,512]{2,1,0:T(1,128)S(1)}, f32[128,1,512]{2,1,0:T(1,128)}, u32[]{:S(2)}) copy-start(f32[128,1,512]{2,1,0:T(1,128)} %broadcast_in_dim_reshape.6) | copy-start | bytes 786436
  132.7 1.2 copy-start.11
  136.5 8.4 %collective-permute-start.7 = (bf16[16,6,512]{2,1,0:T(8,128)(2,1)S(1)}, bf16[16,6,512]{2,1,0:T(8,128)(2,1)S(1)}, u32[]{:S(2)}, u32[]{:S(2)}) collective-permute-start(bf16[16,6,512]{2,1,0:T(8,128)(2,1)S(1)} %pad_maximum_fusion.2), channel_id=1, source_target_pairs={{0,16},{16,0},{1,17},{17,1},{2,18},{18,2},{3,19},{19,3},{4,20},{20... | collective-permute-start | bytes 294920 | tf_op jit(solution)/shard_map/ppermute | solution.py:28
  145.6 24.9 %all-to-all-start.3 = ((bf16[16,6,512]{2,1,0:T(8,128)(2,1)}), bf16[16,6,512]{2,1,0:T(8,128)(2,1)S(1)}, u32[]{:S(2)}, u32[]{:S(2)}) async-start(bf16[16,6,512]{2,1,0:T(8,128)(2,1)} %fusion.15), calls=%async_computation.3 | async-start | bytes 262144 | tf_op jit(solution)/shard_map/all_to_all | solution.py:209
  155.1 20.3 %collective-permute-start.9 = (f32[6,1536]{1,0:T(8,128)S(1)}, f32[6,1536]{1,0:T(8,128)S(1)}, u32[]{:S(2)}, u32[]{:S(2)}) collective-permute-start(f32[6,1536]{1,0:T(8,128)S(1)} %slice.55), channel_id=1, source_target_pairs={{1,0},{2,1},{3,2},{4,3},{5,4},{6,5},{7,6},{8,7},{9,8},{10,9},{11,1... | collective-permute-start | bytes 110600 | tf_op jit(solution)/shard_map/ppermute | solution.py:24
  171.2 17.0 %all-to-all-start.4 = ((f32[16,2,512]{2,1,0:T(2,128)}), f32[16,2,512]{2,1,0:T(2,128)S(1)}, u32[]{:S(2)}, u32[]{:S(2)}) async-start(f32[16,2,512]{2,1,0:T(2,128)} %broadcast_in_dim.54), calls=%async_computation.4 | async-start | bytes 131072 | tf_op jit(solution)/shard_map/all_to_all | solution.py:212
  176.7 5.2 %copy-start.18 = (f32[3,7,512]{2,1,0:T(8,128)S(1)}, f32[3,7,512]{2,1,0:T(8,128)}, u32[]{:S(2)}) copy-start(f32[3,7,512]{2,1,0:T(8,128)} %param.6) | copy-start | bytes 129028
  176.7 5.2 %copy-start.19 = (pred[8,17]{0,1:T(8,128)(4,1)S(1)}, pred[8,17]{0,1:T(8,128)(4,1)}, u32[]{:S(2)}) copy-start(pred[8,17]{0,1:T(8,128)(4,1)} %constant.51) | copy-start | bytes 412
  176.9 10.1 %collective-permute-start.8 = (bf16[128,256]{1,0:T(8,128)(2,1)S(1)}, bf16[128,256]{1,0:T(8,128)(2,1)S(1)}, u32[]{:S(2)}, u32[]{:S(2)}) collective-permute-start(bf16[128,256]{1,0:T(8,128)(2,1)S(1)} %reduce_sum.21), channel_id=1, source_target_pairs={{0,0},{1,1},{2,2},{3,3},{4,4},{5,5},{6,6},{7,7},{8,8},{9,9},{10,10... | collective-permute-start | bytes 196616 | tf_op jit(solution)/shard_map/ppermute | solution.py:216
Sparse Core Ops, SparseCore 0:
  10.1 85.8 all-gather.2
  99.4 82.5 reduce-scatter.1

commit v4 on v3

--- a/solution.py
+++ b/solution.py
@@ -178,17 +178,18 @@
     )
     gated_grad = part_kept + swapped(part_given, "yh").astype(F32)
 
+    query_grad = gated_grad * long_mix
+    mixed_grad = gated_grad * query_side
+    mixed_rim = passed_along(mixed_grad.astype(BF16), -1).astype(F32)[: reach_long - 1]
+
     (out_part,) = call(
         layer_out_kernel,
         [shaped((ZS, rows, 2 * WIDE), BF16)],
         MATMUL,
-        [after(gated_both, proj_part), gathered],
+        [after(gated_both, mixed_grad), gathered],
     )
     out_terms = lax.all_to_all(out_part, FSDP, 0, 0, tiled=True)
 
-    query_grad = gated_grad * long_mix
-    mixed_grad = gated_grad * query_side
-    mixed_rim = passed_along(mixed_grad.astype(BF16), -1).astype(F32)[: reach_long - 1]
     long_part = depthwise(product_ext, mixed_grad)[::-1].reshape(2, ZS, taps_here, channels)
     mixed_ext = jnp.concatenate([mixed_grad, after(mixed_rim, out_part, long_part)], axis=0)
     product_grad = depthwise(mixed_ext, long_taps)
@@ -208,12 +209,12 @@
     terms, out_terms = lax.optimization_barrier((terms, out_terms))
     sums = jnp.sum(lax.all_to_all(terms, ALONG, 0, 0, tiled=True).astype(F32), axis=0)
     grad_long = sums[:taps_here]
-    short_copies = jnp.broadcast_to(sums[None, taps_here:], (ZS, 2, channels))
-    short_sum = lax.all_to_all(short_copies, ALONG, 0, 0, tiled=True).reshape(2 * ZS, channels)
-    grad_short = jnp.transpose(short_sum[: 3 * reach_short].reshape(reach_short, 3, channels), (1, 0, 2))
-
     out_sum = jnp.sum(out_terms.astype(F32), axis=0).astype(BF16)
     layer_out = lax.ppermute(out_sum, AXES, owner_pairs())
+    short_copies = jnp.broadcast_to(sums[None, taps_here:].astype(BF16), (ZS, 2, channels))
+    short_copies = after(short_copies, out_sum, grad_qkv)
+    short_sum = lax.all_to_all(short_copies, ALONG, 0, 0, tiled=True).astype(F32).reshape(2 * ZS, channels)
+    grad_short = jnp.transpose(short_sum[: 3 * reach_short].reshape(reach_short, 3, channels), (1, 0, 2))
     return (layer_out, grad_qkv, grad_short, grad_long, grad_proj)
 
 

time: 198 us -> 195 us (0.985)
  other arithmetic: 5.31 us -> 2.8 us
    ppermute x4, waiting for transfers between devices: 13.5 us -> 7.33 us  [passed_along(): lax.ppermute(value, CTX, [(source, source + steps) for source in range(fi...]
    ppermute x5, waiting for transfers between devices: 8.78 us -> 13.9 us  [swapped(): return lax.ppermute(value, axis, [(0, 1), (1, 0)])]
    all_to_all x1, starting transfers between devices: 9.46 us -> 4.83 us  [local(): lax.all_to_all(terms, ALONG, 0, 0, tiled=True).astype(F32)]
    ppermute x5, starting transfers between devices: 19.6 us -> 23.7 us  [swapped(): return lax.ppermute(value, axis, [(0, 1), (1, 0)])]
    unnamed x48 -> x42, local copies, waits for them, and re-layouts: 8.84 us -> 9.64 us
  transfers between devices with their start and end apart: 17 -> 17, of which waited for: 9 -> 9; matrix products, arithmetic and copies ran while one was open for 16% -> 14% of each run, Pallas kernels for 2% -> 2%
where the time goes in v4:
time: 195 us; the launch traced here: 193 us
  starting transfers between devices  75.2 us (39%)
  waiting for transfers between devices  63.3 us (32%)
  local copies, waits for them, and re-layouts  19.4 us (10%)
  between operations  14.8 us (8%)
  matrix products  12.7 us (7%)
  Pallas kernels  4.8 us (2%)
  other arithmetic  2.8 us (1%)
    ppermute x5, starting transfers between devices, swapped(): return lax.ppermute(value, axis, [(0, 1), (1, 0)])  23.7 us
    all_to_all x1, starting transfers between devices, local(): taps_all = lax.all_to_all(taps_copies, ALONG, 0, 0, tiled=True)  17 us
    all_to_all x1, waiting for transfers between devices, local(): taps_all = lax.all_to_all(taps_copies, ALONG, 0, 0, tiled=True)  14.1 us
    ppermute x5, waiting for transfers between devices, swapped(): return lax.ppermute(value, axis, [(0, 1), (1, 0)])  13.9 us
    all_to_all x1, waiting for transfers between devices, local(): lax.all_to_all(terms, ALONG, 0, 0, tiled=True).astype(F32)  13.3 us
    conv_general_dilated x6, matrix products, depthwise(): lax.conv_general_dilated(padded[None], kernel[:, None, :], (1,), 'VALID',...  12.7 us
    ppermute x4, starting transfers between devices, passed_along(): lax.ppermute(value, CTX, [(source, source + steps) for source in range(fi...  10.3 us
    unnamed x42, local copies, waits for them, and re-layouts  9.64 us
  transfers between devices with their start and end apart: 17, of which 9 were waited for; matrix products, arithmetic and copies ran while one was open for 14% of the time, Pallas kernels for 2%

profile of v4, /device:TPU:6, one launch (start us, length us, event | category | flops | bytes accessed | tf_op | source)
XLA Modules:
  0.0 193.2 jit_solution(9697589715032369419)
XLA Ops:
  7.2 0.7 all-gather.3.cloned.1.call-update
  7.9 5.1 %collective-permute-start.2 = (f32[4,512]{1,0:T(4,128)}, f32[4,512]{1,0:T(4,128)S(1)}, u32[]{:S(2)}, u32[]{:S(2)}) collective-permute-start(f32[4,512]{1,0:T(4,128)} %param.7), channel_id=1, source_target_pairs={{0,16},{16,0},{1,17},{17,1},{2,18},{18,2},{3,19},{19,3},{4,20},{20... | collective-permute-start | bytes 24584 | tf_op jit(solution)/shard_map/ppermute | solution.py:28
  13.0 0.7 slice.38
  14.0 3.8 %collective-permute-start = (bf16[6,1536]{0,1:T(8,128)(2,1)S(1)}, bf16[6,1536]{0,1:T(8,128)(2,1)S(1)}, u32[]{:S(2)}, u32[]{:S(2)}) collective-permute-start(bf16[6,1536]{0,1:T(8,128)(2,1)S(1)} %bitcast.92), channel_id=1, source_target_pairs={{0,1},{1,2},{2,3},{3,4},{4,5},{5,6},{6,7},{7,8},{8,9},{9,10},{10,1... | collective-permute-start | bytes 55304 | tf_op jit(solution)/shard_map/ppermute | solution.py:24
  17.9 0.7 select_bitcast_fusion.3
  18.6 7.3 %collective-permute-done = bf16[6,1536]{0,1:T(8,128)(2,1)S(1)} collective-permute-done((bf16[6,1536]{0,1:T(8,128)(2,1)S(1)}, bf16[6,1536]{0,1:T(8,128)(2,1)S(1)}, u32[]{:S(2)}, u32[]{:S(2)}) %collective-permute-start) | collective-permute-done | bytes 18464 | tf_op jit(solution)/shard_map/ppermute | solution.py:24
  25.9 0.8 broadcast_in_dim.48
  26.7 17.0 %all-to-all-start = ((f32[16,2,4,512]{3,2,1,0:T(4,128)}), f32[16,2,4,512]{3,2,1,0:T(4,128)S(1)}, u32[]{:S(2)}, u32[]{:S(2)}) async-start(f32[16,2,4,512]{3,2,1,0:T(4,128)} %broadcast_in_dim.48), calls=%async_computation | async-start | bytes 524288 | tf_op jit(solution)/shard_map/all_to_all | solution.py:139
  44.6 0.9 copy.60
  45.6 0.9 copy-done.7
  46.4 1.6 fusion.26
  48.2 3.8 %collective-permute-start.1 = (f32[127,512]{1,0:T(8,128)S(1)}, f32[127,512]{1,0:T(8,128)S(1)}, u32[]{:S(2)}, u32[]{:S(2)}) collective-permute-start(f32[127,512]{1,0:T(8,128)S(1)} %slice.54), channel_id=1, source_target_pairs={{0,1},{1,2},{2,3},{3,4},{4,5},{5,6},{6,7},{7,8},{8,9},{9,10},{10,1... | collective-permute-start | bytes 780296 | tf_op jit(solution)/shard_map/ppermute | solution.py:24
  52.2 14.1 %all-to-all-done = f32[16,2,4,512]{3,2,1,0:T(4,128)S(1)} async-done(((f32[16,2,4,512]{3,2,1,0:T(4,128)}), f32[16,2,4,512]{3,2,1,0:T(4,128)S(1)}, u32[]{:S(2)}, u32[]{:S(2)}) %all-to-all-start) | async-done | bytes 262176 | tf_op jit(solution)/shard_map/all_to_all | solution.py:139
  66.3 1.2 broadcast_in_dim.47
  67.5 4.8 %all-to-all-start.1 = ((bf16[16,128,256]{1,2,0:T(8,128)(2,1)}), bf16[16,128,256]{1,2,0:T(8,128)(2,1)S(1)}, u32[]{:S(2)}, u32[]{:S(2)}) async-start(bf16[16,128,256]{1,2,0:T(8,128)(2,1)} %broadcast_in_dim.47), calls=%async_computation.1 | async-start | bytes 2097152 | tf_op jit(solution)/shard_map/all_to_all | solution.py:144
  72.7 2.9 %fusion.11 = f32[1,128,512]{2,0,1:T(1,128)S(1)} fusion(f32[1,255,512]{2,1,0:T(8,128)S(1)} %maximum_bitcast_fusion.3, f32[128,1,512]{2,0,1:T(8,128)S(1)} %bitcast.93), kind=kOutput, calls=%fused_computation.23 | convolution fusion | flops 100663296 | bytes 1046528 | tf_op jit(solution)/shard_map/conv_general_dilated | solution.py:42
  75.7 7.9 %all-to-all-done.1 = bf16[16,128,256]{1,2,0:T(8,128)(2,1)S(1)} async-done(((bf16[16,128,256]{1,2,0:T(8,128)(2,1)}), bf16[16,128,256]{1,2,0:T(8,128)(2,1)S(1)}, u32[]{:S(2)}, u32[]{:S(2)}) %all-to-all-start.1) | async-done | bytes 1048608 | tf_op jit(solution)/shard_map/all_to_all | solution.py:144
  83.6 1.9 collective-permute-start.3
  85.6 3.7 %collective-permute-start.4 = (bf16[128,512]{1,0:T(8,128)(2,1)S(1)}, bf16[128,512]{1,0:T(8,128)(2,1)S(1)}, u32[]{:S(2)}, u32[]{:S(2)}) collective-permute-start(bf16[128,512]{1,0:T(8,128)(2,1)S(1)} %fusion.16), channel_id=1, source_target_pairs={{0,16},{16,0},{1,17},{17,1},{2,18},{18,2},{3,19},{19,3},{4,20},{20... | collective-permute-start | bytes 393224 | tf_op jit(solution)/shard_map/ppermute | solution.py:28
  89.3 5.6 %collective-permute-done.4 = bf16[128,512]{1,0:T(8,128)(2,1)S(1)} collective-permute-done((bf16[128,512]{1,0:T(8,128)(2,1)S(1)}, bf16[128,512]{1,0:T(8,128)(2,1)S(1)}, u32[]{:S(2)}, u32[]{:S(2)}) %collective-permute-start.4) | collective-permute-done | bytes 131104 | tf_op jit(solution)/shard_map/ppermute | solution.py:28
  95.8 1.3 shard_map.92
  97.2 2.0 %copy-done = f32[16,512,128]{2,1,0:T(8,128)} copy-done((f32[16,512,128]{2,1,0:T(8,128)}, f32[16,512,128]{2,1,0:T(8,128)S(1)}, u32[]{:S(2)}) %copy-start) | copy-done | bytes 4194328
  99.2 1.6 copy-done.1
  100.8 1.2 shard_map.93
  102.0 3.8 %collective-permute-start.5 = (bf16[128,512]{1,0:T(8,128)(2,1)S(1)}, bf16[128,512]{1,0:T(8,128)(2,1)S(1)}, u32[]{:S(2)}, u32[]{:S(2)}) collective-permute-start(bf16[128,512]{1,0:T(8,128)(2,1)S(1)} %get-tuple-element.20), channel_id=1, source_target_pairs={{0,16},{16,0},{1,17},{17,1},{2,18},{18,2},{3,19},{19,3},{4,20},{20... | collective-permute-start | bytes 393224 | tf_op jit(solution)/shard_map/ppermute | solution.py:28
  105.9 1.1 broadcast_in_dim_reshape.6
  106.9 3.7 %collective-permute-done.5 = bf16[128,512]{1,0:T(8,128)(2,1)S(1)} collective-permute-done((bf16[128,512]{1,0:T(8,128)(2,1)S(1)}, bf16[128,512]{1,0:T(8,128)(2,1)S(1)}, u32[]{:S(2)}, u32[]{:S(2)}) %collective-permute-start.5) | collective-permute-done | bytes 131104 | tf_op jit(solution)/shard_map/ppermute | solution.py:28
  110.8 1.3 collective-permute-start.6
  112.1 2.9 %fusion.13 = f32[1,128,512]{2,0,1:T(1,128)S(1)} fusion(f32[1,255,512]{2,1,0:T(8,128)S(1)} %copy-done.10, f32[128,1,512]{2,0,1:T(8,128)S(1)} %bitcast.91), kind=kOutput, calls=%fused_computation.25 | convolution fusion | flops 100663296 | bytes 1046528 | tf_op jit(solution)/shard_map/conv_general_dilated | solution.py:42
  115.0 2.3 %shard_map.94 = bf16[16,128,256]{2,1,0:T(8,128)(2,1)} custom-call(bf16[256,512]{1,0:T(8,128)(2,1)S(1)} %bitcast.78, bf16[16,512,128]{2,1,0:T(8,128)(2,1)S(1)} %bitcast.76), custom_call_target="tpu_custom_call" | custom-call | flops 536870912 | bytes 3407872 | tf_op jit(solution)/shard_map/pallas_call | solution.py:105
  117.5 5.6 %all-to-all-start.2 = ((bf16[16,128,256]{2,1,0:T(8,128)(2,1)}), bf16[16,128,256]{2,1,0:T(8,128)(2,1)S(1)}, u32[]{:S(2)}, u32[]{:S(2)}) async-start(bf16[16,128,256]{2,1,0:T(8,128)(2,1)} %shard_map.94), calls=%async_computation.2 | async-start | bytes 2097152 | tf_op jit(solution)/shard_map/all_to_all | solution.py:191
  123.3 0.8 copy-done.12
  124.1 2.8 %fusion.9 = f32[1,128,512]{2,0,1:T(1,128)S(1)} fusion(f32[128,1,512]{2,1,0:T(1,128)S(1)} %copy-done.12, f32[1,255,512]{2,1,0:T(8,128)S(1)} %maximum_bitcast_fusion.4), kind=kOutput, calls=%fused_computation.21 | convolution fusion | flops 100663296 | bytes 1046528 | tf_op jit(solution)/shard_map/conv_general_dilated | solution.py:42
  127.1 1.0 copy-done.8
  128.1 2.1 %fusion.5 = f32[1,7,1536]{2,0,1:T(1,128)S(1)} fusion(bf16[1,134,1536]{2,0,1:T(2,128)(2,1)S(1)} %copy-done.8, f32[128,1,1536]{2,0,1:T(8,128)S(1)} %get-tuple-element.49), kind=kOutput, calls=%fused_computation.12 | convolution fusion | flops 16515072 | bytes 1241088 | tf_op jit(solution)/shard_map/conv_general_dilated | solution.py:42
  130.7 9.2 %collective-permute-start.7 = (bf16[16,6,512]{2,1,0:T(8,128)(2,1)S(1)}, bf16[16,6,512]{2,1,0:T(8,128)(2,1)S(1)}, u32[]{:S(2)}, u32[]{:S(2)}) collective-permute-start(bf16[16,6,512]{2,1,0:T(8,128)(2,1)S(1)} %pad_maximum_fusion.2), channel_id=1, source_target_pairs={{0,16},{16,0},{1,17},{17,1},{2,18},{18,2},{3,19},{19,3},{4,20},{20... | collective-permute-start | bytes 294920 | tf_op jit(solution)/shard_map/ppermute | solution.py:28
  140.0 1.3 collective-permute-start.9
  141.3 4.6 %collective-permute-done.7 = bf16[16,6,512]{2,1,0:T(8,128)(2,1)S(1)} collective-permute-done((bf16[16,6,512]{2,1,0:T(8,128)(2,1)S(1)}, bf16[16,6,512]{2,1,0:T(8,128)(2,1)S(1)}, u32[]{:S(2)}, u32[]{:S(2)}) %collective-permute-start.7) | collective-permute-done | bytes 98336 | tf_op jit(solution)/shard_map/ppermute | solution.py:28
  145.8 0.7 fusion.15
  146.6 4.8 %all-to-all-start.3 = ((bf16[16,6,512]{2,1,0:T(8,128)(2,1)}), bf16[16,6,512]{2,1,0:T(8,128)(2,1)S(1)}, u32[]{:S(2)}, u32[]{:S(2)}) async-start(bf16[16,6,512]{2,1,0:T(8,128)(2,1)} %fusion.15), calls=%async_computation.3 | async-start | bytes 262144 | tf_op jit(solution)/shard_map/all_to_all | solution.py:210
  151.6 1.0 reshape.77
  152.7 0.7 copy-done.15
  154.5 13.3 %all-to-all-done.3 = bf16[16,6,512]{2,1,0:T(8,128)(2,1)S(1)} async-done(((bf16[16,6,512]{2,1,0:T(8,128)(2,1)}), bf16[16,6,512]{2,1,0:T(8,128)(2,1)S(1)}, u32[]{:S(2)}, u32[]{:S(2)}) %all-to-all-start.3) | async-done | bytes 98336 | tf_op jit(solution)/shard_map/all_to_all | solution.py:210
  168.5 3.9 %all-to-all-start.4 = ((bf16[16,2,512]{2,1,0:T(2,128)(2,1)}), bf16[16,2,512]{2,1,0:T(2,128)(2,1)S(1)}, u32[]{:S(2)}, u32[]{:S(2)}) async-start(bf16[16,2,512]{2,1,0:T(2,128)(2,1)} %broadcast_in_dim.54), calls=%async_computation.4 | async-start | bytes 65536 | tf_op jit(solution)/shard_map/all_to_all | solution.py:216
  172.5 5.0 %collective-permute-start.8 = (bf16[128,256]{1,0:T(8,128)(2,1)S(1)}, bf16[128,256]{1,0:T(8,128)(2,1)S(1)}, u32[]{:S(2)}, u32[]{:S(2)}) collective-permute-start(bf16[128,256]{1,0:T(8,128)(2,1)S(1)} %reduce_sum.21), channel_id=1, source_target_pairs={{0,0},{1,1},{2,2},{3,3},{4,4},{5,5},{6,6},{7,7},{8,8},{9,9},{10,10... | collective-permute-start | bytes 196616 | tf_op jit(solution)/shard_map/ppermute | solution.py:213
  177.4 0.9 copy.77
  178.4 4.2 %collective-permute-done.8 = bf16[128,256]{1,0:T(8,128)(2,1)S(1)} collective-permute-done((bf16[128,256]{1,0:T(8,128)(2,1)S(1)}, bf16[128,256]{1,0:T(8,128)(2,1)S(1)}, u32[]{:S(2)}, u32[]{:S(2)}) %collective-permute-start.8) | collective-permute-done | bytes 65568 | tf_op jit(solution)/shard_map/ppermute | solution.py:213
  183.1 1.9 all-to-all-done.4
  (97 shorter events, 7.8 us)
Async XLA Ops:
  7.2 36.5 %copy-start.11 = (bf16[128,3,512]{2,0,1:T(8,128)(2,1)S(1)}, bf16[128,3,512]{2,0,1:T(8,128)(2,1)}, u32[]{:S(2)}) copy-start(bf16[128,3,512]{2,0,1:T(8,128)(2,1)} %param.5) | copy-start | bytes 1179652
  7.2 36.7 %copy-start.14 = (f32[3,7,512]{2,1,0:T(8,128)S(1)}, f32[3,7,512]{2,1,0:T(8,128)}, u32[]{:S(2)}) copy-start(f32[3,7,512]{2,1,0:T(8,128)} %param.6) | copy-start | bytes 129028
  7.2 92.0 %all-gather.3.cloned.1.call-start = ((), (), s32[]{:S(2)}) async-start(), calls=%async_computation.7 | async-start | bytes 2228224 | tf_op jit(solution)/shard_map/all_gather | solution.py:134
  7.9 10.0 %collective-permute-start.2 = (f32[4,512]{1,0:T(4,128)}, f32[4,512]{1,0:T(4,128)S(1)}, u32[]{:S(2)}, u32[]{:S(2)}) collective-permute-start(f32[4,512]{1,0:T(4,128)} %param.7), channel_id=1, source_target_pairs={{0,16},{16,0},{1,17},{17,1},{2,18},{18,2},{3,19},{19,3},{4,20},{20... | collective-permute-start | bytes 24584 | tf_op jit(solution)/shard_map/ppermute | solution.py:28
  14.0 11.9 %collective-permute-start = (bf16[6,1536]{0,1:T(8,128)(2,1)S(1)}, bf16[6,1536]{0,1:T(8,128)(2,1)S(1)}, u32[]{:S(2)}, u32[]{:S(2)}) collective-permute-start(bf16[6,1536]{0,1:T(8,128)(2,1)S(1)} %bitcast.92), channel_id=1, source_target_pairs={{0,1},{1,2},{2,3},{3,4},{4,5},{5,6},{6,7},{7,8},{8,9},{9,10},{10,1... | collective-permute-start | bytes 55304 | tf_op jit(solution)/shard_map/ppermute | solution.py:24
  26.7 39.6 %all-to-all-start = ((f32[16,2,4,512]{3,2,1,0:T(4,128)}), f32[16,2,4,512]{3,2,1,0:T(4,128)S(1)}, u32[]{:S(2)}, u32[]{:S(2)}) async-start(f32[16,2,4,512]{3,2,1,0:T(4,128)} %broadcast_in_dim.48), calls=%async_computation | async-start | bytes 524288 | tf_op jit(solution)/shard_map/all_to_all | solution.py:139
  45.5 0.9 copy-start.7
  48.1 4.0 %copy-start.13 = (bf16[128,256]{1,0:T(8,128)(2,1)S(1)}, bf16[128,256]{1,0:T(8,128)(2,1)}, u32[]{:S(2)}) copy-start(bf16[128,256]{1,0:T(8,128)(2,1)} %param.9) | copy-start | bytes 196612
  48.2 24.2 %collective-permute-start.1 = (f32[127,512]{1,0:T(8,128)S(1)}, f32[127,512]{1,0:T(8,128)S(1)}, u32[]{:S(2)}, u32[]{:S(2)}) collective-permute-start(f32[127,512]{1,0:T(8,128)S(1)} %slice.54), channel_id=1, source_target_pairs={{0,1},{1,2},{2,3},{3,4},{4,5},{5,6},{6,7},{7,8},{8,9},{9,10},{10,1... | collective-permute-start | bytes 780296 | tf_op jit(solution)/shard_map/ppermute | solution.py:24
  67.5 16.1 %all-to-all-start.1 = ((bf16[16,128,256]{1,2,0:T(8,128)(2,1)}), bf16[16,128,256]{1,2,0:T(8,128)(2,1)S(1)}, u32[]{:S(2)}, u32[]{:S(2)}) async-start(bf16[16,128,256]{1,2,0:T(8,128)(2,1)} %broadcast_in_dim.47), calls=%async_computation.1 | async-start | bytes 2097152 | tf_op jit(solution)/shard_map/all_to_all | solution.py:144
  72.3 113.4 %reduce-scatter.2.cloned.1.call-start = ((), (), s32[]{:S(2)}) async-start(), calls=%async_computation.6 | async-start | bytes 4456448 | tf_op jit(solution)/shard_map/reduce_scatter | solution.py:167
  72.4 3.2 %copy-start.9 = (f32[1,255,512]{2,1,0:T(8,128)}, f32[1,255,512]{2,1,0:T(8,128)S(1)}, u32[]{:S(2)}) copy-start(f32[1,255,512]{2,1,0:T(8,128)S(1)} %maximum_bitcast_fusion.3) | copy-start | bytes 1566724
  72.5 3.2 %copy-start.3 = (f32[2,16,4,512]{3,2,1,0:T(4,128)}, f32[2,16,4,512]{3,2,1,0:T(4,128)S(1)}, u32[]{:S(2)}) copy-start(f32[2,16,4,512]{3,2,1,0:T(4,128)S(1)} %copy.63) | copy-start | bytes 786436
  75.7 19.3 %copy-start.5 = (f32[1,128,512]{2,0,1:T(1,128)}, f32[1,128,512]{2,0,1:T(1,128)S(1)}, u32[]{:S(2)}) copy-start(f32[1,128,512]{2,0,1:T(1,128)S(1)} %fusion.11) | copy-start | bytes 786436
  83.6 11.3 %collective-permute-start.3 = (bf16[8,128,256]{1,2,0:T(8,128)(2,1)S(1)}, bf16[8,128,256]{1,2,0:T(8,128)(2,1)S(1)}, u32[]{:S(2)}, u32[]{:S(2)}) collective-permute-start(bf16[8,128,256]{1,2,0:T(8,128)(2,1)S(1)} %dynamic-slice_bitcast_fusion), channel_id=1, source_target_pairs={{0,32},{32,0},{1,33},{33,1},{2,34},{34,2},{3,35},{35,3},{4,36},{36... | collective-permute-start | bytes 1572872 | tf_op jit(solution)/shard_map/ppermute | solution.py:28
  85.6 9.3 %collective-permute-start.4 = (bf16[128,512]{1,0:T(8,128)(2,1)S(1)}, bf16[128,512]{1,0:T(8,128)(2,1)S(1)}, u32[]{:S(2)}, u32[]{:S(2)}) collective-permute-start(bf16[128,512]{1,0:T(8,128)(2,1)S(1)} %fusion.16), channel_id=1, source_target_pairs={{0,16},{16,0},{1,17},{17,1},{2,18},{18,2},{3,19},{19,3},{4,20},{20... | collective-permute-start | bytes 393224 | tf_op jit(solution)/shard_map/ppermute | solution.py:28
  97.1 2.0 %copy-start = (f32[16,512,128]{2,1,0:T(8,128)}, f32[16,512,128]{2,1,0:T(8,128)S(1)}, u32[]{:S(2)}) copy-start(f32[16,512,128]{2,1,0:T(8,128)S(1)} %shard_map.92) | copy-start | bytes 12582916
  99.2 1.6 copy-start.1
  100.8 5.1 %copy-start.4 = (f32[2,16,4,512]{3,2,1,0:T(4,128)S(1)}, f32[2,16,4,512]{3,2,1,0:T(4,128)}, u32[]{:S(2)}) copy-start(f32[2,16,4,512]{3,2,1,0:T(4,128)} %copy-done.3) | copy-start | bytes 786436
  100.8 9.9 %copy-start.6 = (f32[1,128,512]{2,0,1:T(1,128)S(1)}, f32[1,128,512]{2,0,1:T(1,128)}, u32[]{:S(2)}) copy-start(f32[1,128,512]{2,0,1:T(1,128)} %copy-done.5) | copy-start | bytes 786436
  102.0 10.1 %copy-start.10 = (f32[1,255,512]{2,1,0:T(8,128)S(1)}, f32[1,255,512]{2,1,0:T(8,128)}, u32[]{:S(2)}) copy-start(f32[1,255,512]{2,1,0:T(8,128)} %copy-done.9) | copy-start | bytes 1566724
  102.0 8.6 %collective-permute-start.5 = (bf16[128,512]{1,0:T(8,128)(2,1)S(1)}, bf16[128,512]{1,0:T(8,128)(2,1)S(1)}, u32[]{:S(2)}, u32[]{:S(2)}) collective-permute-start(bf16[128,512]{1,0:T(8,128)(2,1)S(1)} %get-tuple-element.20), channel_id=1, source_target_pairs={{0,16},{16,0},{1,17},{17,1},{2,18},{18,2},{3,19},{19,3},{4,20},{20... | collective-permute-start | bytes 393224 | tf_op jit(solution)/shard_map/ppermute | solution.py:28
  110.8 12.4 %collective-permute-start.6 = (bf16[128,512]{1,0:T(8,128)(2,1)S(1)}, bf16[128,512]{1,0:T(8,128)(2,1)S(1)}, u32[]{:S(2)}, u32[]{:S(2)}) collective-permute-start(bf16[128,512]{1,0:T(8,128)(2,1)S(1)} %get-tuple-element.42), channel_id=1, source_target_pairs={{1,0},{2,1},{3,2},{4,3},{5,4},{6,5},{7,6},{8,7},{9,8},{10,9},{11,1... | collective-permute-start | bytes 393224 | tf_op jit(solution)/shard_map/ppermute | solution.py:24
  112.1 2.9 %copy-start.2 = (bf16[8192,128]{1,0:T(8,128)(2,1)S(1)}, bf16[8192,128]{1,0:T(8,128)(2,1)}, u32[]{:S(2)}) copy-start(bf16[8192,128]{1,0:T(8,128)(2,1)} %all-gather.3.cloned.1.call-done) | copy-start | bytes 6291460
  117.5 29.1 %all-to-all-start.2 = ((bf16[16,128,256]{2,1,0:T(8,128)(2,1)}), bf16[16,128,256]{2,1,0:T(8,128)(2,1)S(1)}, u32[]{:S(2)}, u32[]{:S(2)}) async-start(bf16[16,128,256]{2,1,0:T(8,128)(2,1)} %shard_map.94), calls=%async_computation.2 | async-start | bytes 2097152 | tf_op jit(solution)/shard_map/all_to_all | solution.py:191
  123.1 1.0 copy-start.12
  126.9 1.2 copy-start.8
  130.7 15.1 %collective-permute-start.7 = (bf16[16,6,512]{2,1,0:T(8,128)(2,1)S(1)}, bf16[16,6,512]{2,1,0:T(8,128)(2,1)S(1)}, u32[]{:S(2)}, u32[]{:S(2)}) collective-permute-start(bf16[16,6,512]{2,1,0:T(8,128)(2,1)S(1)} %pad_maximum_fusion.2), channel_id=1, source_target_pairs={{0,16},{16,0},{1,17},{17,1},{2,18},{18,2},{3,19},{19,3},{4,20},{20... | collective-permute-start | bytes 294920 | tf_op jit(solution)/shard_map/ppermute | solution.py:28
  140.0 11.5 %collective-permute-start.9 = (f32[6,1536]{1,0:T(8,128)S(1)}, f32[6,1536]{1,0:T(8,128)S(1)}, u32[]{:S(2)}, u32[]{:S(2)}) collective-permute-start(f32[6,1536]{1,0:T(8,128)S(1)} %slice.57), channel_id=1, source_target_pairs={{1,0},{2,1},{3,2},{4,3},{5,4},{6,5},{7,6},{8,7},{9,8},{10,9},{11,1... | collective-permute-start | bytes 110600 | tf_op jit(solution)/shard_map/ppermute | solution.py:24
  146.6 21.2 %all-to-all-start.3 = ((bf16[16,6,512]{2,1,0:T(8,128)(2,1)}), bf16[16,6,512]{2,1,0:T(8,128)(2,1)S(1)}, u32[]{:S(2)}, u32[]{:S(2)}) async-start(bf16[16,6,512]{2,1,0:T(8,128)(2,1)} %fusion.15), calls=%async_computation.3 | async-start | bytes 262144 | tf_op jit(solution)/shard_map/all_to_all | solution.py:210
  152.6 0.8 copy-start.15
  152.6 0.8 copy-start.16
  168.5 16.5 %all-to-all-start.4 = ((bf16[16,2,512]{2,1,0:T(2,128)(2,1)}), bf16[16,2,512]{2,1,0:T(2,128)(2,1)S(1)}, u32[]{:S(2)}, u32[]{:S(2)}) async-start(bf16[16,2,512]{2,1,0:T(2,128)(2,1)} %broadcast_in_dim.54), calls=%async_computation.4 | async-start | bytes 65536 | tf_op jit(solution)/shard_map/all_to_all | solution.py:216
  172.5 10.1 %collective-permute-start.8 = (bf16[128,256]{1,0:T(8,128)(2,1)S(1)}, bf16[128,256]{1,0:T(8,128)(2,1)S(1)}, u32[]{:S(2)}, u32[]{:S(2)}) collective-permute-start(bf16[128,256]{1,0:T(8,128)(2,1)S(1)} %reduce_sum.21), channel_id=1, source_target_pairs={{0,0},{1,1},{2,2},{3,3},{4,4},{5,5},{6,6},{7,7},{8,8},{9,9},{10,10... | collective-permute-start | bytes 196616 | tf_op jit(solution)/shard_map/ppermute | solution.py:213
Sparse Core Ops, SparseCore 0:
  10.1 85.8 all-gather.2
  99.4 80.4 reduce-scatter.1
